TPU v7x, 512 devices: a whole 4x4x16 slice. The times are simulated.
512 devices in a mesh: tm: 4 (over z_hi, core), space: 128 (over z_lo, y, x).
Axes of the slice: x: 4, y: 4, z: 16 (z_hi: 2, z_lo: 8; z = z_hi * 8 + z_lo), core: 2. Of those that a mesh axis runs over, the one named last changes fastest.
Arguments:
- initial: float32 [256, 64, 256], P('space'), may hold values from -1 to 1
- guess: float32 [4, 256, 64, 256], P('tm', 'space'), may hold values from -1 to 1
Outputs:
- states: float32 [4, 256, 64, 256], P('tm', 'space')
All inputs are finite; a program needn't handle non-finite values.
Results may differ from a plain program's by a relative error of at most 0.0001.
Values sent between devices are 32-bit elements; how exact they have to be, the bound alone decides.
A program may use at most 64 MiB of HBM per device.

v0:
```python
import jax
import jax.numpy as jnp
from jax import lax
from jax.sharding import PartitionSpec as P

ITERS = 2


time_step = 0.24
half_step = 0.12


def padded_2(block, sides, width):
    for axis, dim in sides:
        count = lax.axis_size(axis)
        forward = [(i, i + 1) for i in range(count - 1)]
        forward.append((count - 1, 0))
        backward = [(target, source) for source, target in forward]
        low = lax.ppermute(
            lax.slice_in_dim(block, block.shape[dim] - width, None, axis=dim), axis, forward
        )
        high = lax.ppermute(lax.slice_in_dim(block, 0, width, axis=dim), axis, backward)
        block = jnp.concatenate([low, block, high], axis=dim)
    return block


def passed_along(x, axis, by):
    count = lax.axis_size(axis)
    pairs = [(i, i + by) for i in range(count) if 0 <= i + by < count]
    return lax.ppermute(x, axis, pairs)


def plane_sum(field, padded, axis_one, axis_two):
    total = padded
    total = total + jnp.roll(field, 1, axis_one) + jnp.roll(field, -1, axis_one)
    total = total + jnp.roll(field, 1, axis_two) + jnp.roll(field, -1, axis_two)
    return total - 6.0 * field


def fine_force(field):
    padded = padded_2(field, (("space", 0),), 1)
    lapl = plane_sum(field, padded[2:] + padded[:-2], 1, 2)
    return lapl + field - field * field * field


def coarse_force(field):
    padded = padded_2(field, (("space", 0),), 1)
    lapl = plane_sum(field, padded[2:] + padded[:-2], 1, 2)
    return 0.25 * lapl + field - field * field * field


def restrict(field):
    depth, rows, cols = field.shape
    blocks = field.reshape(depth // 2, 2, rows // 2, 2, cols // 2, 2)
    return jnp.mean(blocks, axis=(1, 3, 5))


def prolong(field):
    field = jnp.repeat(field, 2, axis=0)
    field = jnp.repeat(field, 2, axis=1)
    return jnp.repeat(field, 2, axis=2)


def advance(forces, start, force_fn):
    first_int = time_step * (
        5.0 / 24.0 * forces[0] + 1.0 / 3.0 * forces[1] - 1.0 / 24.0 * forces[2]
    )
    second_int = time_step * (
        -1.0 / 24.0 * forces[0] + 1.0 / 3.0 * forces[1] + 5.0 / 24.0 * forces[2]
    )
    node_one = start + half_step * (force_fn(start) - forces[0]) + first_int
    node_two = node_one + half_step * (force_fn(node_one) - forces[1]) + second_int
    return [start, node_one, node_two]


def local(initial, guess):
    slice_count = lax.axis_size("tm")
    position = lax.axis_index("tm")
    leading = position == 0
    current = guess[0]
    nodes = [current, current, current]
    coarse_init = restrict(initial)
    for iteration in range(ITERS):
        previous = passed_along(nodes[2], "tm", 1)
        fine_start = jnp.where(leading, initial, previous)
        restricted = [restrict(value) for value in nodes]
        forces = [coarse_force(value) for value in restricted]
        start = coarse_init
        for round_index in range(slice_count):
            swept = advance(forces, start, coarse_force)
            if round_index + 1 < slice_count:
                arrived = passed_along(swept[2], "tm", 1)
                start = jnp.where(leading, coarse_init, arrived)
        corrected = [
            nodes[number] + prolong(swept[number] - restricted[number]) for number in range(3)
        ]
        fine_forces = [fine_force(value) for value in corrected]
        nodes = advance(fine_forces, fine_start, fine_force)
    return nodes[2][None]


def solution(mesh):
    return jax.shard_map(
        local,
        mesh=mesh,
        in_specs=(P("space", None, None), P("tm", "space", None, None)),
        out_specs=P("tm", "space", None, None),
        check_vma=False,
    )
```

profile of v0, /device:TPU:1, one launch (start us, length us, event | category | flops | bytes accessed | tf_op | source)
XLA Modules:
  0.0 624.0 jit_solution(549211544592896514)
XLA Ops:
  0.0 16.8 %collective-permute-start = (f32[2,64,256]{2,1,0:T(8,128)}, f32[2,64,256]{2,1,0:T(8,128)S(1)}, u32[]{:S(2)}, u32[]{:S(2)}) collective-permute-start(f32[2,64,256]{2,1,0:T(8,128)} %bitcast.106), channel_id=1, source_target_pairs={{0,128},{128,256},{256,384},{1,129},{129,257},{257,385},{2,130},{1... | collective-permute-start | bytes 393224 | tf_op jit(solution)/shard_map/ppermute | solution.py:30
  46.8 14.2 %collective-permute-start.3 = (f32[1,32,128]{2,1,0:T(8,128)S(1)}, f32[1,32,128]{2,1,0:T(8,128)S(1)}, u32[]{:S(2)}, u32[]{:S(2)}) collective-permute-start(f32[1,32,128]{2,1,0:T(8,128)S(1)} %multiply_bitcast_fusion.4), channel_id=1, source_target_pairs={{1,0},{2,1},{3,2},{4,3},{5,4},{6,5},{7,6},{8,7},{9,8},{10,9},{11,1... | collective-permute-start | bytes 49160 | tf_op jit(solution)/shard_map/ppermute | solution.py:22
  88.1 13.4 %collective-permute-done.8 = f32[1,32,128]{2,1,0:T(8,128)S(1)} collective-permute-done((f32[1,32,128]{2,1,0:T(8,128)S(1)}, f32[1,32,128]{2,1,0:T(8,128)S(1)}, u32[]{:S(2)}, u32[]{:S(2)}) %collective-permute-start.8) | collective-permute-done | bytes 16416 | tf_op jit(solution)/shard_map/ppermute | solution.py:19
  112.3 11.9 %collective-permute-done.11 = f32[1,32,128]{2,1,0:T(8,128)S(1)} collective-permute-done((f32[1,32,128]{2,1,0:T(8,128)S(1)}, f32[1,32,128]{2,1,0:T(8,128)S(1)}, u32[]{:S(2)}, u32[]{:S(2)}) %collective-permute-start.11) | collective-permute-done | bytes 16416 | tf_op jit(solution)/shard_map/ppermute | solution.py:19
  129.8 11.9 %collective-permute-done.13 = f32[1,32,128]{2,1,0:T(8,128)S(1)} collective-permute-done((f32[1,32,128]{2,1,0:T(8,128)S(1)}, f32[1,32,128]{2,1,0:T(8,128)S(1)}, u32[]{:S(2)}, u32[]{:S(2)}) %collective-permute-start.13) | collective-permute-done | bytes 16416 | tf_op jit(solution)/shard_map/ppermute | solution.py:19
  141.8 15.2 %collective-permute-start.14 = (f32[1,32,128]{2,1,0:T(8,128)S(1)}, f32[1,32,128]{2,1,0:T(8,128)S(1)}, u32[]{:S(2)}, u32[]{:S(2)}) collective-permute-start(f32[1,32,128]{2,1,0:T(8,128)S(1)} %fusion.113), channel_id=1, source_target_pairs={{0,128},{128,256},{256,384},{1,129},{129,257},{257,385},{2,130},{1... | collective-permute-start | bytes 49160 | tf_op jit(solution)/shard_map/ppermute | solution.py:30
  163.3 11.9 %collective-permute-done.16 = f32[1,32,128]{2,1,0:T(8,128)S(1)} collective-permute-done((f32[1,32,128]{2,1,0:T(8,128)S(1)}, f32[1,32,128]{2,1,0:T(8,128)S(1)}, u32[]{:S(2)}, u32[]{:S(2)}) %collective-permute-start.16) | collective-permute-done | bytes 16416 | tf_op jit(solution)/shard_map/ppermute | solution.py:19
  180.8 11.9 %collective-permute-done.18 = f32[1,32,128]{2,1,0:T(8,128)S(1)} collective-permute-done((f32[1,32,128]{2,1,0:T(8,128)S(1)}, f32[1,32,128]{2,1,0:T(8,128)S(1)}, u32[]{:S(2)}, u32[]{:S(2)}) %collective-permute-start.18) | collective-permute-done | bytes 16416 | tf_op jit(solution)/shard_map/ppermute | solution.py:19
  192.8 15.2 %collective-permute-start.19 = (f32[1,32,128]{2,1,0:T(8,128)S(1)}, f32[1,32,128]{2,1,0:T(8,128)S(1)}, u32[]{:S(2)}, u32[]{:S(2)}) collective-permute-start(f32[1,32,128]{2,1,0:T(8,128)S(1)} %fusion.123), channel_id=1, source_target_pairs={{0,128},{128,256},{256,384},{1,129},{129,257},{257,385},{2,130},{1... | collective-permute-start | bytes 49160 | tf_op jit(solution)/shard_map/ppermute | solution.py:30
  213.5 12.7 %collective-permute-start.22 = (f32[1,32,128]{2,1,0:T(8,128)S(1)}, f32[1,32,128]{2,1,0:T(8,128)S(1)}, u32[]{:S(2)}, u32[]{:S(2)}) collective-permute-start(f32[1,32,128]{2,1,0:T(8,128)S(1)} %get-tuple-element.29), channel_id=1, source_target_pairs={{1,0},{2,1},{3,2},{4,3},{5,4},{6,5},{7,6},{8,7},{9,8},{10,9},{11,1... | collective-permute-start | bytes 49160 | tf_op jit(solution)/shard_map/ppermute | solution.py:22
  228.5 13.1 %collective-permute-done.23 = f32[1,32,128]{2,1,0:T(8,128)S(1)} collective-permute-done((f32[1,32,128]{2,1,0:T(8,128)S(1)}, f32[1,32,128]{2,1,0:T(8,128)S(1)}, u32[]{:S(2)}, u32[]{:S(2)}) %collective-permute-start.23) | collective-permute-done | bytes 16416 | tf_op jit(solution)/shard_map/ppermute | solution.py:19
  265.5 12.7 %collective-permute-start.24 = (f32[1,64,256]{2,1,0:T(8,128)S(1)}, f32[1,64,256]{2,1,0:T(8,128)S(1)}, u32[]{:S(2)}, u32[]{:S(2)}) collective-permute-start(f32[1,64,256]{2,1,0:T(8,128)S(1)} %get-tuple-element.116), channel_id=1, source_target_pairs={{1,0},{2,1},{3,2},{4,3},{5,4},{6,5},{7,6},{8,7},{9,8},{10,9},{11,1... | collective-permute-start | bytes 196616 | tf_op jit(solution)/shard_map/ppermute | solution.py:22
  280.2 14.2 %collective-permute-start.28 = (f32[1,64,256]{2,1,0:T(8,128)S(1)}, f32[1,64,256]{2,1,0:T(8,128)S(1)}, u32[]{:S(2)}, u32[]{:S(2)}) collective-permute-start(f32[1,64,256]{2,1,0:T(8,128)S(1)} %get-tuple-element.106), channel_id=1, source_target_pairs={{1,0},{2,1},{3,2},{4,3},{5,4},{6,5},{7,6},{8,7},{9,8},{10,9},{11,1... | collective-permute-start | bytes 196616 | tf_op jit(solution)/shard_map/ppermute | solution.py:22
  296.3 14.2 %collective-permute-start.35 = (f32[1,32,128]{2,1,0:T(8,128)S(1)}, f32[1,32,128]{2,1,0:T(8,128)S(1)}, u32[]{:S(2)}, u32[]{:S(2)}) collective-permute-start(f32[1,32,128]{2,1,0:T(8,128)S(1)} %multiply_bitcast_fusion.2), channel_id=1, source_target_pairs={{1,0},{2,1},{3,2},{4,3},{5,4},{6,5},{7,6},{8,7},{9,8},{10,9},{11,1... | collective-permute-start | bytes 49160 | tf_op jit(solution)/shard_map/ppermute | solution.py:22
  321.8 14.2 %collective-permute-start.37 = (f32[1,32,128]{2,1,0:T(8,128)S(1)}, f32[1,32,128]{2,1,0:T(8,128)S(1)}, u32[]{:S(2)}, u32[]{:S(2)}) collective-permute-start(f32[1,32,128]{2,1,0:T(8,128)S(1)} %multiply_bitcast_fusion.1), channel_id=1, source_target_pairs={{1,0},{2,1},{3,2},{4,3},{5,4},{6,5},{7,6},{8,7},{9,8},{10,9},{11,1... | collective-permute-start | bytes 49160 | tf_op jit(solution)/shard_map/ppermute | solution.py:22
  368.3 13.3 %collective-permute-done.40 = f32[1,32,128]{2,1,0:T(8,128)S(1)} collective-permute-done((f32[1,32,128]{2,1,0:T(8,128)S(1)}, f32[1,32,128]{2,1,0:T(8,128)S(1)}, u32[]{:S(2)}, u32[]{:S(2)}) %collective-permute-start.40) | collective-permute-done | bytes 16416 | tf_op jit(solution)/shard_map/ppermute | solution.py:19
  433.7 11.9 %collective-permute-done.47 = f32[1,32,128]{2,1,0:T(8,128)S(1)} collective-permute-done((f32[1,32,128]{2,1,0:T(8,128)S(1)}, f32[1,32,128]{2,1,0:T(8,128)S(1)}, u32[]{:S(2)}, u32[]{:S(2)}) %collective-permute-start.47) | collective-permute-done | bytes 16416 | tf_op jit(solution)/shard_map/ppermute | solution.py:19
  445.7 15.2 %collective-permute-start.48 = (f32[1,32,128]{2,1,0:T(8,128)S(1)}, f32[1,32,128]{2,1,0:T(8,128)S(1)}, u32[]{:S(2)}, u32[]{:S(2)}) collective-permute-start(f32[1,32,128]{2,1,0:T(8,128)S(1)} %fusion.153), channel_id=1, source_target_pairs={{0,128},{128,256},{256,384},{1,129},{129,257},{257,385},{2,130},{1... | collective-permute-start | bytes 49160 | tf_op jit(solution)/shard_map/ppermute | solution.py:30
  497.9 14.1 %collective-permute-start.53 = (f32[1,32,128]{2,1,0:T(8,128)S(1)}, f32[1,32,128]{2,1,0:T(8,128)S(1)}, u32[]{:S(2)}, u32[]{:S(2)}) collective-permute-start(f32[1,32,128]{2,1,0:T(8,128)S(1)} %fusion.163), channel_id=1, source_target_pairs={{0,128},{128,256},{256,384},{1,129},{129,257},{257,385},{2,130},{1... | collective-permute-start | bytes 49160 | tf_op jit(solution)/shard_map/ppermute | solution.py:30
  518.1 12.7 %collective-permute-start.56 = (f32[1,32,128]{2,1,0:T(8,128)S(1)}, f32[1,32,128]{2,1,0:T(8,128)S(1)}, u32[]{:S(2)}, u32[]{:S(2)}) collective-permute-start(f32[1,32,128]{2,1,0:T(8,128)S(1)} %get-tuple-element.12), channel_id=1, source_target_pairs={{1,0},{2,1},{3,2},{4,3},{5,4},{6,5},{7,6},{8,7},{9,8},{10,9},{11,1... | collective-permute-start | bytes 49160 | tf_op jit(solution)/shard_map/ppermute | solution.py:22
  533.8 14.2 %collective-permute-start.54 = (f32[1,64,256]{2,1,0:T(8,128)S(1)}, f32[1,64,256]{2,1,0:T(8,128)S(1)}, u32[]{:S(2)}, u32[]{:S(2)}) collective-permute-start(f32[1,64,256]{2,1,0:T(8,128)S(1)} %get-tuple-element.43), channel_id=1, source_target_pairs={{1,0},{2,1},{3,2},{4,3},{5,4},{6,5},{7,6},{8,7},{9,8},{10,9},{11,1... | collective-permute-start | bytes 196616 | tf_op jit(solution)/shard_map/ppermute | solution.py:22
  574.0 14.2 %collective-permute-start.62 = (f32[1,64,256]{2,1,0:T(8,128)S(1)}, f32[1,64,256]{2,1,0:T(8,128)S(1)}, u32[]{:S(2)}, u32[]{:S(2)}) collective-permute-start(f32[1,64,256]{2,1,0:T(8,128)S(1)} %get-tuple-element.53), channel_id=1, source_target_pairs={{1,0},{2,1},{3,2},{4,3},{5,4},{6,5},{7,6},{8,7},{9,8},{10,9},{11,1... | collective-permute-start | bytes 196616 | tf_op jit(solution)/shard_map/ppermute | solution.py:22
  590.2 13.8 %collective-permute-done.63 = f32[1,64,256]{2,1,0:T(8,128)S(1)} collective-permute-done((f32[1,64,256]{2,1,0:T(8,128)S(1)}, f32[1,64,256]{2,1,0:T(8,128)S(1)}, u32[]{:S(2)}, u32[]{:S(2)}) %collective-permute-start.63) | collective-permute-done | bytes 65568 | tf_op jit(solution)/shard_map/ppermute | solution.py:19
  610.7 12.4 %collective-permute-done.65 = f32[1,64,256]{2,1,0:T(8,128)S(1)} collective-permute-done((f32[1,64,256]{2,1,0:T(8,128)S(1)}, f32[1,64,256]{2,1,0:T(8,128)S(1)}, u32[]{:S(2)}, u32[]{:S(2)}) %collective-permute-start.65) | collective-permute-done | bytes 65568 | tf_op jit(solution)/shard_map/ppermute | solution.py:19
  (306 shorter events, 296.8 us)
Async XLA Ops:
  0.0 38.1 %collective-permute-start = (f32[2,64,256]{2,1,0:T(8,128)}, f32[2,64,256]{2,1,0:T(8,128)S(1)}, u32[]{:S(2)}, u32[]{:S(2)}) collective-permute-start(f32[2,64,256]{2,1,0:T(8,128)} %bitcast.106), channel_id=1, source_target_pairs={{0,128},{128,256},{256,384},{1,129},{129,257},{257,385},{2,130},{1... | collective-permute-start | bytes 393224 | tf_op jit(solution)/shard_map/ppermute | solution.py:30
  26.2 45.5 %collective-permute-start.5 = (f32[1,32,128]{2,1,0:T(8,128)S(1)}, f32[1,32,128]{2,1,0:T(8,128)S(1)}, u32[]{:S(2)}, u32[]{:S(2)}) collective-permute-start(f32[1,32,128]{2,1,0:T(8,128)S(1)} %multiply_bitcast_fusion.3), channel_id=1, source_target_pairs={{1,0},{2,1},{3,2},{4,3},{5,4},{6,5},{7,6},{8,7},{9,8},{10,9},{11,1... | collective-permute-start | bytes 49160 | tf_op jit(solution)/shard_map/ppermute | solution.py:22
  36.2 35.5 %collective-permute-start.6 = (f32[1,32,128]{2,1,0:T(8,128)S(1)}, f32[1,32,128]{2,1,0:T(8,128)S(1)}, u32[]{:S(2)}, u32[]{:S(2)}) collective-permute-start(f32[1,32,128]{2,1,0:T(8,128)S(1)} %multiply_bitcast_fusion.3), channel_id=1, source_target_pairs={{0,1},{1,2},{2,3},{3,4},{4,5},{5,6},{6,7},{7,8},{8,9},{9,10},{10,1... | collective-permute-start | bytes 49160 | tf_op jit(solution)/shard_map/ppermute | solution.py:19
  46.8 24.9 %collective-permute-start.3 = (f32[1,32,128]{2,1,0:T(8,128)S(1)}, f32[1,32,128]{2,1,0:T(8,128)S(1)}, u32[]{:S(2)}, u32[]{:S(2)}) collective-permute-start(f32[1,32,128]{2,1,0:T(8,128)S(1)} %multiply_bitcast_fusion.4), channel_id=1, source_target_pairs={{1,0},{2,1},{3,2},{4,3},{5,4},{6,5},{7,6},{8,7},{9,8},{10,9},{11,1... | collective-permute-start | bytes 49160 | tf_op jit(solution)/shard_map/ppermute | solution.py:22
  192.8 20.5 %collective-permute-start.19 = (f32[1,32,128]{2,1,0:T(8,128)S(1)}, f32[1,32,128]{2,1,0:T(8,128)S(1)}, u32[]{:S(2)}, u32[]{:S(2)}) collective-permute-start(f32[1,32,128]{2,1,0:T(8,128)S(1)} %fusion.123), channel_id=1, source_target_pairs={{0,128},{128,256},{256,384},{1,129},{129,257},{257,385},{2,130},{1... | collective-permute-start | bytes 49160 | tf_op jit(solution)/shard_map/ppermute | solution.py:30
  208.1 70.2 %collective-permute-start.1 = (f32[1,64,256]{2,1,0:T(8,128)S(1)}, f32[1,64,256]{2,1,0:T(8,128)S(1)}, u32[]{:S(2)}, u32[]{:S(2)}) collective-permute-start(f32[1,64,256]{2,1,0:T(8,128)S(1)} %get-tuple-element.127), channel_id=1, source_target_pairs={{1,0},{2,1},{3,2},{4,3},{5,4},{6,5},{7,6},{8,7},{9,8},{10,9},{11,1... | collective-permute-start | bytes 196616 | tf_op jit(solution)/shard_map/ppermute | solution.py:22
  210.0 70.2 %collective-permute-start.2 = (f32[1,64,256]{2,1,0:T(8,128)S(1)}, f32[1,64,256]{2,1,0:T(8,128)S(1)}, u32[]{:S(2)}, u32[]{:S(2)}) collective-permute-start(f32[1,64,256]{2,1,0:T(8,128)S(1)} %get-tuple-element.128), channel_id=1, source_target_pairs={{0,1},{1,2},{2,3},{3,4},{4,5},{5,6},{6,7},{7,8},{8,9},{9,10},{10,1... | collective-permute-start | bytes 196616 | tf_op jit(solution)/shard_map/ppermute | solution.py:19
  260.2 34.2 %collective-permute-start.20 = (f32[1,64,256]{2,1,0:T(8,128)S(1)}, f32[1,64,256]{2,1,0:T(8,128)S(1)}, u32[]{:S(2)}, u32[]{:S(2)}) collective-permute-start(f32[1,64,256]{2,1,0:T(8,128)S(1)} %get-tuple-element.93), channel_id=1, source_target_pairs={{1,0},{2,1},{3,2},{4,3},{5,4},{6,5},{7,6},{8,7},{9,8},{10,9},{11,1... | collective-permute-start | bytes 196616 | tf_op jit(solution)/shard_map/ppermute | solution.py:22
  262.1 34.2 %collective-permute-start.21 = (f32[1,64,256]{2,1,0:T(8,128)S(1)}, f32[1,64,256]{2,1,0:T(8,128)S(1)}, u32[]{:S(2)}, u32[]{:S(2)}) collective-permute-start(f32[1,64,256]{2,1,0:T(8,128)S(1)} %get-tuple-element.94), channel_id=1, source_target_pairs={{0,1},{1,2},{2,3},{3,4},{4,5},{5,6},{6,7},{7,8},{8,9},{9,10},{10,1... | collective-permute-start | bytes 196616 | tf_op jit(solution)/shard_map/ppermute | solution.py:19
  265.5 45.1 %collective-permute-start.24 = (f32[1,64,256]{2,1,0:T(8,128)S(1)}, f32[1,64,256]{2,1,0:T(8,128)S(1)}, u32[]{:S(2)}, u32[]{:S(2)}) collective-permute-start(f32[1,64,256]{2,1,0:T(8,128)S(1)} %get-tuple-element.116), channel_id=1, source_target_pairs={{1,0},{2,1},{3,2},{4,3},{5,4},{6,5},{7,6},{8,7},{9,8},{10,9},{11,1... | collective-permute-start | bytes 196616 | tf_op jit(solution)/shard_map/ppermute | solution.py:22
  278.2 34.2 %collective-permute-start.25 = (f32[1,64,256]{2,1,0:T(8,128)S(1)}, f32[1,64,256]{2,1,0:T(8,128)S(1)}, u32[]{:S(2)}, u32[]{:S(2)}) collective-permute-start(f32[1,64,256]{2,1,0:T(8,128)S(1)} %get-tuple-element.117), channel_id=1, source_target_pairs={{0,1},{1,2},{2,3},{3,4},{4,5},{5,6},{6,7},{7,8},{8,9},{9,10},{10,1... | collective-permute-start | bytes 196616 | tf_op jit(solution)/shard_map/ppermute | solution.py:19
  280.2 32.3 %collective-permute-start.28 = (f32[1,64,256]{2,1,0:T(8,128)S(1)}, f32[1,64,256]{2,1,0:T(8,128)S(1)}, u32[]{:S(2)}, u32[]{:S(2)}) collective-permute-start(f32[1,64,256]{2,1,0:T(8,128)S(1)} %get-tuple-element.106), channel_id=1, source_target_pairs={{1,0},{2,1},{3,2},{4,3},{5,4},{6,5},{7,6},{8,7},{9,8},{10,9},{11,1... | collective-permute-start | bytes 196616 | tf_op jit(solution)/shard_map/ppermute | solution.py:22
  296.3 70.0 %collective-permute-start.35 = (f32[1,32,128]{2,1,0:T(8,128)S(1)}, f32[1,32,128]{2,1,0:T(8,128)S(1)}, u32[]{:S(2)}, u32[]{:S(2)}) collective-permute-start(f32[1,32,128]{2,1,0:T(8,128)S(1)} %multiply_bitcast_fusion.2), channel_id=1, source_target_pairs={{1,0},{2,1},{3,2},{4,3},{5,4},{6,5},{7,6},{8,7},{9,8},{10,9},{11,1... | collective-permute-start | bytes 49160 | tf_op jit(solution)/shard_map/ppermute | solution.py:22
  310.5 57.8 %collective-permute-start.36 = (f32[1,32,128]{2,1,0:T(8,128)S(1)}, f32[1,32,128]{2,1,0:T(8,128)S(1)}, u32[]{:S(2)}, u32[]{:S(2)}) collective-permute-start(f32[1,32,128]{2,1,0:T(8,128)S(1)} %multiply_bitcast_fusion.2), channel_id=1, source_target_pairs={{0,1},{1,2},{2,3},{3,4},{4,5},{5,6},{6,7},{7,8},{8,9},{9,10},{10,1... | collective-permute-start | bytes 49160 | tf_op jit(solution)/shard_map/ppermute | solution.py:19
  321.8 46.5 %collective-permute-start.37 = (f32[1,32,128]{2,1,0:T(8,128)S(1)}, f32[1,32,128]{2,1,0:T(8,128)S(1)}, u32[]{:S(2)}, u32[]{:S(2)}) collective-permute-start(f32[1,32,128]{2,1,0:T(8,128)S(1)} %multiply_bitcast_fusion.1), channel_id=1, source_target_pairs={{1,0},{2,1},{3,2},{4,3},{5,4},{6,5},{7,6},{8,7},{9,8},{10,9},{11,1... | collective-permute-start | bytes 49160 | tf_op jit(solution)/shard_map/ppermute | solution.py:22
  341.3 27.0 %collective-permute-start.38 = (f32[1,32,128]{2,1,0:T(8,128)S(1)}, f32[1,32,128]{2,1,0:T(8,128)S(1)}, u32[]{:S(2)}, u32[]{:S(2)}) collective-permute-start(f32[1,32,128]{2,1,0:T(8,128)S(1)} %multiply_bitcast_fusion.1), channel_id=1, source_target_pairs={{0,1},{1,2},{2,3},{3,4},{4,5},{5,6},{6,7},{7,8},{8,9},{9,10},{10,1... | collective-permute-start | bytes 49160 | tf_op jit(solution)/shard_map/ppermute | solution.py:19
  461.0 24.9 %collective-permute-start.32 = (f32[2,64,256]{2,1,0:T(8,128)S(1)}, f32[2,64,256]{2,1,0:T(8,128)S(1)}, u32[]{:S(2)}, u32[]{:S(2)}) collective-permute-start(f32[2,64,256]{2,1,0:T(8,128)S(1)} %get-tuple-element.23), channel_id=1, source_target_pairs={{0,128},{128,256},{256,384},{1,129},{129,257},{257,385},{2,130},{1... | collective-permute-start | bytes 393224 | tf_op jit(solution)/shard_map/ppermute | solution.py:30
  497.9 20.0 %collective-permute-start.53 = (f32[1,32,128]{2,1,0:T(8,128)S(1)}, f32[1,32,128]{2,1,0:T(8,128)S(1)}, u32[]{:S(2)}, u32[]{:S(2)}) collective-permute-start(f32[1,32,128]{2,1,0:T(8,128)S(1)} %fusion.163), channel_id=1, source_target_pairs={{0,128},{128,256},{256,384},{1,129},{129,257},{257,385},{2,130},{1... | collective-permute-start | bytes 49160 | tf_op jit(solution)/shard_map/ppermute | solution.py:30
  512.6 59.5 %collective-permute-start.33 = (f32[1,64,256]{2,1,0:T(8,128)S(1)}, f32[1,64,256]{2,1,0:T(8,128)S(1)}, u32[]{:S(2)}, u32[]{:S(2)}) collective-permute-start(f32[1,64,256]{2,1,0:T(8,128)S(1)} %get-tuple-element.81), channel_id=1, source_target_pairs={{1,0},{2,1},{3,2},{4,3},{5,4},{6,5},{7,6},{8,7},{9,8},{10,9},{11,1... | collective-permute-start | bytes 196616 | tf_op jit(solution)/shard_map/ppermute | solution.py:22
  514.5 59.5 %collective-permute-start.34 = (f32[1,64,256]{2,1,0:T(8,128)S(1)}, f32[1,64,256]{2,1,0:T(8,128)S(1)}, u32[]{:S(2)}, u32[]{:S(2)}) collective-permute-start(f32[1,64,256]{2,1,0:T(8,128)S(1)} %get-tuple-element.82), channel_id=1, source_target_pairs={{0,1},{1,2},{2,3},{3,4},{4,5},{5,6},{6,7},{7,8},{8,9},{9,10},{10,1... | collective-permute-start | bytes 196616 | tf_op jit(solution)/shard_map/ppermute | solution.py:19
  518.1 30.0 %collective-permute-start.56 = (f32[1,32,128]{2,1,0:T(8,128)S(1)}, f32[1,32,128]{2,1,0:T(8,128)S(1)}, u32[]{:S(2)}, u32[]{:S(2)}) collective-permute-start(f32[1,32,128]{2,1,0:T(8,128)S(1)} %get-tuple-element.12), channel_id=1, source_target_pairs={{1,0},{2,1},{3,2},{4,3},{5,4},{6,5},{7,6},{8,7},{9,8},{10,9},{11,1... | collective-permute-start | bytes 49160 | tf_op jit(solution)/shard_map/ppermute | solution.py:22
  533.8 54.4 %collective-permute-start.54 = (f32[1,64,256]{2,1,0:T(8,128)S(1)}, f32[1,64,256]{2,1,0:T(8,128)S(1)}, u32[]{:S(2)}, u32[]{:S(2)}) collective-permute-start(f32[1,64,256]{2,1,0:T(8,128)S(1)} %get-tuple-element.43), channel_id=1, source_target_pairs={{1,0},{2,1},{3,2},{4,3},{5,4},{6,5},{7,6},{8,7},{9,8},{10,9},{11,1... | collective-permute-start | bytes 196616 | tf_op jit(solution)/shard_map/ppermute | solution.py:22
  555.3 34.8 %collective-permute-start.55 = (f32[1,64,256]{2,1,0:T(8,128)S(1)}, f32[1,64,256]{2,1,0:T(8,128)S(1)}, u32[]{:S(2)}, u32[]{:S(2)}) collective-permute-start(f32[1,64,256]{2,1,0:T(8,128)S(1)} %get-tuple-element.44), channel_id=1, source_target_pairs={{0,1},{1,2},{2,3},{3,4},{4,5},{5,6},{6,7},{7,8},{8,9},{9,10},{10,1... | collective-permute-start | bytes 196616 | tf_op jit(solution)/shard_map/ppermute | solution.py:19
  565.5 24.6 %collective-permute-start.58 = (f32[1,64,256]{2,1,0:T(8,128)}, f32[1,64,256]{2,1,0:T(8,128)S(1)}, u32[]{:S(2)}, u32[]{:S(2)}) collective-permute-start(f32[1,64,256]{2,1,0:T(8,128)} %get-tuple-element.63), channel_id=1, source_target_pairs={{1,0},{2,1},{3,2},{4,3},{5,4},{6,5},{7,6},{8,7},{9,8},{10,9},{11,1... | collective-permute-start | bytes 196616 | tf_op jit(solution)/shard_map/ppermute | solution.py:22
  (44 other events, 711.5 us)
where the time goes:
time: 626 us; the launch traced here: 624 us
  starting transfers between devices  356 us (57%)
  waiting for transfers between devices  210 us (34%)
  local copies, waits for them, and re-layouts  36.7 us (6%)
  other arithmetic  19.2 us (3%)
    ppermute x29, waiting for transfers between devices, padded_2(): lax.ppermute(lax.slice_in_dim(block, block.shape[dim] - width, None, axis...  208 us
    ppermute x29, starting transfers between devices, padded_2(): lax.ppermute(lax.slice_in_dim(block, 0, width, axis=dim), axis, backward)  183 us
    ppermute x8, starting transfers between devices, passed_along(): return lax.ppermute(x, axis, pairs)  93.7 us
    ppermute x29, starting transfers between devices, padded_2(): lax.ppermute(lax.slice_in_dim(block, block.shape[dim] - width, None, axis...  78.9 us
    reduce_sum x5, local copies, waits for them, and re-layouts, restrict(): return jnp.mean(blocks, axis=(1, 3, 5))  28 us
    reduce_sum x9, other arithmetic, restrict(): return jnp.mean(blocks, axis=(1, 3, 5))  15.6 us
  transfers between devices with their start and end apart: 66, of which 21 were waited for; matrix products, arithmetic and copies ran while one was open for 8% of the time, Pallas kernels for 0%

commit v1 on v0

v1 whole, which is shorter than its diff:
```python
import functools

import jax
import jax.numpy as jnp
from jax import lax
from jax.experimental import pallas as pl
from jax.experimental.pallas import tpu as pltpu
from jax.sharding import PartitionSpec as P

MESH = pl.DeviceIdType.MESH
DT, H = 0.24, 0.12
A = (DT * 5.0 / 24.0 - H, DT / 3.0, -DT / 24.0)
B = (-DT / 24.0, DT / 3.0 - H, DT * 5.0 / 24.0)
REACH = 9
DEEP = 5


def split(x):
    high = x.astype(jnp.bfloat16)
    rest = x - high.astype(jnp.float32)
    mid = rest.astype(jnp.bfloat16)
    low = (rest - mid.astype(jnp.float32)).astype(jnp.bfloat16)
    return jnp.concatenate([high, mid, low], axis=0)


def permuted(x, perm):
    rows = x.shape[0]
    out = jnp.dot(split(x), perm, preferred_element_type=jnp.float32)
    return out[:rows] + (out[rows : 2 * rows] + out[2 * rows :])


def perm_matrix(to_parity):
    i = lax.broadcasted_iota(jnp.int32, (256, 256), 0)
    j = lax.broadcasted_iota(jnp.int32, (256, 256), 1)
    wide, packed = (i, j) if to_parity else (j, i)
    lane = jnp.where(packed < 128, 2 * packed, 2 * packed - 255)
    return jnp.where(wide == lane, 1.0, 0.0).astype(jnp.bfloat16)


def lane_roll(x, by):
    return pltpu.roll(x, by % 128, 1)


def row_roll(x, by):
    return pltpu.roll(x, by % 32, 0)


def coarse_sum(below, x, above):
    total = below + above
    total = total + lane_roll(x, 1) + lane_roll(x, -1)
    return total + row_roll(x, 1) + row_roll(x, -1)


def euler(below, x, above):
    return 0.25 * H * coarse_sum(below, x, above) + x * ((1.0 - 0.5 * H) - H * (x * x))


def cube(x):
    return x * x * x


def mix(weights, values):
    return weights[0] * values[0] + weights[1] * values[1] + weights[2] * values[2]


def sub(ref, plane, part):
    return ref[plane, 32 * part : 32 * part + 32, :]


def restricted(ref, first):
    total = None
    for plane in (first, first + 1):
        for part in range(4):
            piece = sub(ref, plane, part)
            total = piece if total is None else total + piece
    return 0.125 * total


def fine_sum(ref, plane, part):
    row, col = part // 2, part % 2
    beside = sub(ref, plane, row * 2 + 1 - col)
    over = sub(ref, plane, (1 - row) * 2 + col)
    total = sub(ref, plane - 1, part) + sub(ref, plane + 1, part)
    total = total + beside + lane_roll(beside, 1 if col == 0 else -1)
    return total + over + row_roll(over, 1 if row == 0 else -1)


def fine_sweep(nodes, shifts, start, z1, z2, q1, q2, d2, out1, first1, out2, first2):
    for plane in range(6):
        for part in range(4):
            rows = slice(32 * part, 32 * part + 32)
            u = [sub(nodes[m], plane, part) + shifts[m][plane // 2] for m in range(3)]
            n0 = sub(start, plane, part)
            z = H * n0 + mix(A, u)
            z1[plane, rows, :] = z
            if 1 <= plane <= 4:
                cubes = [cube(v) for v in u]
                q1[plane, rows, :] = n0 - 5.0 * z - (H * cube(n0) + mix(A, cubes))
                d2[plane, rows, :] = mix(B, u)
                if 2 <= plane <= 3:
                    q2[plane, rows, :] = mix(B, cubes)
    for plane in range(1, 5):
        for part in range(4):
            rows = slice(32 * part, 32 * part + 32)
            n1 = sub(q1, plane, part) + fine_sum(z1, plane, part)
            z = H * n1 + sub(d2, plane, part)
            z2[plane, rows, :] = z
            if 2 <= plane <= 3:
                if out1 is not None:
                    out1[first1 + plane - 2, rows, :] = n1
                q2[plane, rows, :] = n1 - 5.0 * z - (H * cube(n1) + sub(q2, plane, part))
    for plane in range(2, 4):
        for part in range(4):
            rows = slice(32 * part, 32 * part + 32)
            out2[first2 + plane - 2, rows, :] = sub(q2, plane, part) + fine_sum(z2, plane, part)


def kernel(
    ns, nt,
    init_ref, guess_ref, out_ref,
    g, f, n1, n2, f2,
    z1, z2, q1, q2, d2,
    ic, sa, sb, w, v, c1, c2, s, t1, t2, halves,
    ssem, rsem,
):
    t = lax.axis_index("tm")
    c = lax.axis_index("space")
    even = lax.rem(t, 2) == 0

    def at(by):
        return (t, lax.rem(c + by + ns, ns))

    up = (jnp.minimum(t + 1, nt - 1), c)
    down = (jnp.maximum(t - 1, 0), c)

    barrier = pltpu.get_barrier_semaphore()
    for by in range(1, REACH + 1):
        for sign in (1, -1):
            pl.semaphore_signal(barrier, inc=1, device_id=at(sign * by), device_id_type=MESH)

    @pl.when(t > 0)
    def _():
        pl.semaphore_signal(barrier, inc=1, device_id=down, device_id_type=MESH)

    @pl.when(t < nt - 1)
    def _():
        pl.semaphore_signal(barrier, inc=1, device_id=up, device_id_type=MESH)

    rows = jnp.concatenate([guess_ref[0, 0], guess_ref[0, 1], init_ref[0], init_ref[1]], axis=0)
    packed = permuted(rows, perm_matrix(True))
    halves[0] = packed[:, :128]
    halves[1] = packed[:, 128:]
    for plane in range(2):
        for row in range(2):
            for col in range(2):
                part = slice(64 * row + 32 * col, 64 * row + 32 * col + 32)
                g[2 + plane, part, :] = halves[col, pl.ds(64 * plane + row, 32, stride=2), :]
                q1[2 + plane, part, :] = halves[col, pl.ds(128 + 64 * plane + row, 32, stride=2), :]
    own = restricted(q1, 2)
    ic[REACH] = own

    @pl.when(t == 0)
    def _():
        f[2:4] = q1[2:4]
        f2[2:4] = q1[2:4]

    pl.semaphore_wait(barrier, 2 * REACH + jnp.where((t > 0) & (t < nt - 1), 2, 1))

    ids = iter(range(200))

    def message(src, dst, number, device):
        return pltpu.make_async_remote_copy(
            src_ref=src, dst_ref=dst, send_sem=ssem.at[number], recv_sem=rsem.at[number],
            device_id=device, device_id_type=MESH,
        )

    def start(copies):
        for copy in copies:
            copy.start()

    def arrive(copies):
        for copy in copies:
            copy.wait_recv()

    def sent(copies):
        for copy in copies:
            copy.wait_send()

    def halo(ref):
        return [
            message(ref.at[pl.ds(2, 2)], ref.at[pl.ds(0, 2)], next(ids), at(1)),
            message(ref.at[pl.ds(2, 2)], ref.at[pl.ds(4, 2)], next(ids), at(-1)),
        ]

    def spread(ref, middle, far, near=1):
        out = []
        for by in range(near, far + 1):
            for sign in (1, -1):
                out.append(message(ref.at[middle], ref.at[middle - sign * by], next(ids), at(sign * by)))
        return out

    ic_near = spread(ic, REACH, 5)
    ic_mid = spread(ic, REACH, 7, 6)
    ic_far = spread(ic, REACH, 9, 8)
    g_up = message(g.at[pl.ds(2, 2)], f.at[pl.ds(2, 2)], next(ids), up)
    g_halo = halo(g)
    f_halo = halo(f)
    v_near = spread(v, DEEP, 3)
    v_far = spread(v, DEEP, 5, 4)
    n1_halo = halo(n1)
    n2_halo = halo(n2)
    n2_up = message(n2.at[pl.ds(2, 2)], f2.at[pl.ds(2, 2)], next(ids), up)
    f2_halo = halo(f2)
    s_core = message(t2.at[pl.ds(2, 7)], s.at[pl.ds(2, 7)], next(ids), up)
    s_cross = message(t2.at[DEEP], s.at[DEEP], next(ids), up)
    s_spread = spread(s, DEEP, 5)

    @pl.when(t < nt - 1)
    def _():
        g_up.start()

    start(ic_near)

    @pl.when(t >= 2)
    def _():
        start(ic_mid)

    @pl.when(t == 3)
    def _():
        start(ic_far)

    start(g_halo)

    @pl.when(t == 0)
    def _():
        start(f_halo)

    @pl.when(lax.rem(t, 2) == 1)
    def _():
        g_up.wait_recv()
        start(f_halo)

    arrive(ic_near)

    @pl.when(t >= 2)
    def _():
        arrive(ic_mid)

    @pl.when(t == 3)
    def _():
        arrive(ic_far)

    @pl.when(t < 2)
    def _():
        for j in (*range(REACH - 5), *range(REACH + 6, 2 * REACH + 1)):
            ic[j] = own

    @pl.when(t == 2)
    def _():
        for j in (0, 1, 2 * REACH - 1, 2 * REACH):
            ic[j] = own

    for j in range(2 * REACH + 1):
        sa[j] = ic[j]

    sb[0] = own
    sb[2 * REACH] = own

    def two_steps(_, carry):
        for j in range(1, 2 * REACH):
            sb[j] = euler(sa[j - 1], sa[j], sa[j + 1])
        for j in range(2, 2 * REACH - 1):
            sa[j] = euler(sb[j - 1], sb[j], sb[j + 1])
        return carry

    lax.fori_loop(0, t, two_steps, 0)
    for j in range(REACH - 2, REACH + 3):
        sb[j] = euler(sa[j - 1], sa[j], sa[j + 1])
    for j in range(3):
        k = REACH - 1 + j
        w[0, j] = sa[k]
        w[1, j] = sb[k]
        w[2, j] = euler(sb[k - 1], sb[k], sb[k + 1])

    @pl.when(t == 2)
    def _():
        g_up.wait_recv()
        start(f_halo)

    arrive(g_halo)
    arrive(f_halo)
    old = [restricted(g, 2 * j) for j in range(3)]
    shifts = [[w[m, j] - old[j] for j in range(3)] for m in range(3)]
    fine_sweep((g, g, g), shifts, f, z1, z2, q1, q2, d2, n1, 2, n2, 2)

    v[DEEP, 0] = restricted(f, 2)
    v[DEEP, 1] = restricted(n1, 2)
    v[DEEP, 2] = restricted(n2, 2)
    start(v_near)

    @pl.when(even)
    def _():
        start(v_far)

    @pl.when(t < nt - 1)
    def _():
        n2_up.start()

    start(n1_halo)
    start(n2_halo)

    @pl.when(t == 0)
    def _():
        f2[0:2] = f[0:2]
        f2[4:6] = f[4:6]
        for j in range(2 * DEEP + 1):
            s[j] = ic[REACH - DEEP + j]

    @pl.when(lax.rem(t, 2) == 1)
    def _():
        n2_up.wait_recv()
        start(f2_halo)

    arrive(v_near)

    @pl.when(even)
    def _():
        arrive(v_far)

    def forcing(weights, out, j):
        z = [mix(weights, [v[k, m] for m in range(3)]) for k in (j - 1, j, j + 1)]
        cubes = mix(weights, [cube(v[j, m]) for m in range(3)])
        out[j] = 0.25 * coarse_sum(*z) - 0.5 * z[1] - cubes

    def forcings(reach):
        for j in range(DEEP - reach, DEEP + reach + 1):
            forcing(A, c1, j)
            if abs(j - DEEP) < reach:
                forcing(B, c2, j)

    def chain(reach):
        for j in range(DEEP - reach, DEEP + reach + 1):
            t1[j] = euler(s[j - 1], s[j], s[j + 1]) + c1[j]
        for j in range(DEEP - reach + 1, DEEP + reach):
            t2[j] = euler(t1[j - 1], t1[j], t1[j + 1]) + c2[j]

    @pl.when(even)
    def _():
        forcings(4)

    @pl.when(jnp.logical_not(even))
    def _():
        forcings(2)

    @pl.when(t == 2)
    def _():
        n2_up.wait_recv()
        start(f2_halo)
        s_cross.wait_recv()
        start(s_spread)
        arrive(s_spread)

    @pl.when(even)
    def _():
        chain(4)
        s_core.start()

    @pl.when(jnp.logical_not(even))
    def _():
        s_core.wait_recv()
        chain(2)

    @pl.when(t == 1)
    def _():
        s_cross.start()

    arrive(n1_halo)
    arrive(n2_halo)

    @pl.when(t > 0)
    def _():
        arrive(f2_halo)

    shifts = []
    for m, level in enumerate((s, t1, t2)):
        shifts.append([level[DEEP - 1 + j] - v[DEEP - 1 + j, m] for j in range(3)])
    fine_sweep((f, n1, n2), shifts, f2, z1, z2, q1, q2, d2, None, 0, out_ref, 0)

    sent(ic_near)
    sent(g_halo)
    sent(f_halo)
    sent(v_near)
    sent(n1_halo)
    sent(n2_halo)

    @pl.when(t >= 2)
    def _():
        sent(ic_mid)

    @pl.when(t == 3)
    def _():
        sent(ic_far)

    @pl.when(t < nt - 1)
    def _():
        g_up.wait_send()
        n2_up.wait_send()

    @pl.when(t > 0)
    def _():
        sent(f2_halo)

    @pl.when(even)
    def _():
        sent(v_far)
        s_core.wait_send()

    @pl.when(t == 1)
    def _():
        s_cross.wait_send()

    @pl.when(t == 2)
    def _():
        sent(s_spread)


def interleave(x_ref, out_ref, halves):
    for plane in range(2):
        for row in range(2):
            for col in range(2):
                halves[col, pl.ds(64 * plane + row, 32, stride=2), :] = sub(x_ref, plane, 2 * row + col)
    wide = permuted(jnp.concatenate([halves[0], halves[1]], axis=1), perm_matrix(False))
    out_ref[0, 0] = wide[:64]
    out_ref[0, 1] = wide[64:]


def solution(mesh):
    ns, nt = mesh.shape["space"], mesh.shape["tm"]
    vmem = pl.BlockSpec(memory_space=pltpu.VMEM)

    def local(initial, guess):
        slab6 = pltpu.VMEM((6, 128, 128), jnp.float32)

        def planes(*lead):
            return pltpu.VMEM((*lead, 32, 128), jnp.float32)

        last = pl.pallas_call(
            functools.partial(kernel, ns, nt),
            out_shape=jax.ShapeDtypeStruct((2, 128, 128), jnp.float32),
            in_specs=[vmem, vmem],
            out_specs=vmem,
            scratch_shapes=[slab6] * 10
            + [planes(2 * REACH + 1)] * 3
            + [planes(3, 3), planes(2 * DEEP + 1, 3)]
            + [planes(2 * DEEP + 1)] * 5
            + [pltpu.VMEM((2, 256, 128), jnp.float32)]
            + [pltpu.SemaphoreType.DMA((64,)), pltpu.SemaphoreType.DMA((64,))],
            compiler_params=pltpu.CompilerParams(
                collective_id=0, has_side_effects=True, vmem_limit_bytes=32 << 20
            ),
            name="pfasst",
        )(initial, guess)
        return pl.pallas_call(
            interleave,
            out_shape=jax.ShapeDtypeStruct(guess.shape, jnp.float32),
            in_specs=[vmem],
            out_specs=vmem,
            scratch_shapes=[pltpu.VMEM((2, 128, 128), jnp.float32)],
            compiler_params=pltpu.CompilerParams(vmem_limit_bytes=32 << 20),
            name="interleave",
        )(last)

    return jax.shard_map(
        local,
        mesh=mesh,
        in_specs=(P("space", None, None), P("tm", "space", None, None)),
        out_specs=P("tm", "space", None, None),
        check_vma=False,
    )
```

time: 626 us -> 66.9 us (0.11)
  the two profiles are of different devices: /device:TPU:1 before, /device:TPU:257 now
where the time goes in v1:
time: 66.9 us; the launch traced here: 66.8 us
  Pallas kernels  65 us (97%)
  local copies, waits for them, and re-layouts  1.81 us (3%)
    pallas_call x1, Pallas kernels, local(): pl.pallas_call(functools.partial(kernel, ns, nt), out_shape=jax.ShapeDtyp...  64.1 us
    unnamed x4, local copies, waits for them, and re-layouts  1.81 us

profile of v1, /device:TPU:257, one launch (start us, length us, event | category | flops | bytes accessed | tf_op | source)
XLA Modules:
  0.0 66.8 jit_solution(8702060804589890271)
XLA Ops:
  0.0 0.0 copy-start
  0.0 0.9 %copy-done = f32[2,64,256]{2,1,0:T(8,128)S(1)} copy-done((f32[2,64,256]{2,1,0:T(8,128)S(1)}, f32[2,64,256]{2,1,0:T(8,128)}, u32[]{:S(2)}) %copy-start) | copy-done | bytes 131096
  0.9 0.0 copy-start.1
  0.9 0.9 %copy-done.1 = f32[1,2,64,256]{3,2,1,0:T(8,128)S(1)} copy-done((f32[1,2,64,256]{3,2,1,0:T(8,128)S(1)}, f32[1,2,64,256]{3,2,1,0:T(8,128)}, u32[]{:S(2)}) %copy-start.1) | copy-done | bytes 131096
  1.8 64.1 %pfasst.1.x_ref = f32[2,128,128]{2,1,0:T(8,128)S(1)} custom-call(f32[2,64,256]{2,1,0:T(8,128)S(1)} %copy-done, f32[1,2,64,256]{3,2,1,0:T(8,128)S(1)} %copy-done.1), custom_call_target="tpu_custom_call" | custom-call | tf_op jit(solution)/shard_map/pfasst/pallas_call | solution.py:447
  65.9 0.9 %interleave.1 = f32[1,2,64,256]{3,2,1,0:T(8,128)} custom-call(f32[2,128,128]{2,1,0:T(8,128)S(1)} %pfasst.1.x_ref), custom_call_target="tpu_custom_call" | custom-call | tf_op jit(solution)/shard_map/interleave/pallas_call | solution.py:463
Async XLA Ops:
  0.0 0.9 %copy-start = (f32[2,64,256]{2,1,0:T(8,128)S(1)}, f32[2,64,256]{2,1,0:T(8,128)}, u32[]{:S(2)}) copy-start(f32[2,64,256]{2,1,0:T(8,128)} %init_ref.1) | copy-start | bytes 393220
  0.9 0.9 %copy-start.1 = (f32[1,2,64,256]{3,2,1,0:T(8,128)S(1)}, f32[1,2,64,256]{3,2,1,0:T(8,128)}, u32[]{:S(2)}) copy-start(f32[1,2,64,256]{3,2,1,0:T(8,128)} %guess_ref.1) | copy-start | bytes 393220

commit v2 on v1

v2 whole, which is shorter than its diff:
```python
import functools

import jax
import jax.numpy as jnp
from jax import lax
from jax.experimental import pallas as pl
from jax.experimental.pallas import tpu as pltpu
from jax.sharding import PartitionSpec as P

MESH = pl.DeviceIdType.MESH
DT, H = 0.24, 0.12
A = (DT * 5.0 / 24.0 - H, DT / 3.0, -DT / 24.0)
B = (-DT / 24.0, DT / 3.0 - H, DT * 5.0 / 24.0)
REACH = 9
DEEP = 5


def split(x):
    high = x.astype(jnp.bfloat16)
    rest = x - high.astype(jnp.float32)
    mid = rest.astype(jnp.bfloat16)
    low = (rest - mid.astype(jnp.float32)).astype(jnp.bfloat16)
    return jnp.concatenate([high, mid, low], axis=0)


def permuted(x, perm):
    rows = x.shape[0]
    out = jnp.dot(split(x), perm, preferred_element_type=jnp.float32)
    return out[:rows] + (out[rows : 2 * rows] + out[2 * rows :])


def perm_matrix(to_parity):
    i = lax.broadcasted_iota(jnp.int32, (256, 256), 0)
    j = lax.broadcasted_iota(jnp.int32, (256, 256), 1)
    wide, packed = (i, j) if to_parity else (j, i)
    lane = jnp.where(packed < 128, 2 * packed, 2 * packed - 255)
    return jnp.where(wide == lane, 1.0, 0.0).astype(jnp.bfloat16)


def lane_roll(x, by):
    return pltpu.roll(x, by % 128, 1)


def row_roll(x, by):
    return pltpu.roll(x, by % 32, 0)


def coarse_sum(below, x, above):
    total = below + above
    total = total + lane_roll(x, 1) + lane_roll(x, -1)
    return total + row_roll(x, 1) + row_roll(x, -1)


def euler(below, x, above):
    return 0.25 * H * coarse_sum(below, x, above) + x * ((1.0 - 0.5 * H) - H * (x * x))


def cube(x):
    return x * x * x


def mix(weights, values):
    return weights[0] * values[0] + weights[1] * values[1] + weights[2] * values[2]


def sub(ref, plane, part):
    return ref[plane, 32 * part : 32 * part + 32, :]


def restricted(ref, first):
    total = None
    for plane in (first, first + 1):
        for part in range(4):
            piece = sub(ref, plane, part)
            total = piece if total is None else total + piece
    return 0.125 * total


def fine_sum(ref, plane, part):
    row, col = part // 2, part % 2
    beside = sub(ref, plane, row * 2 + 1 - col)
    over = sub(ref, plane, (1 - row) * 2 + col)
    total = sub(ref, plane - 1, part) + sub(ref, plane + 1, part)
    total = total + beside + lane_roll(beside, 1 if col == 0 else -1)
    return total + over + row_roll(over, 1 if row == 0 else -1)


def fine_sweep(nodes, shifts, start, z1, z2, q1, q2, d2, out1, first1, out2, first2):
    for plane in range(6):
        for part in range(4):
            rows = slice(32 * part, 32 * part + 32)
            u = [sub(nodes[m], plane, part) + shifts[m][plane // 2] for m in range(3)]
            n0 = sub(start, plane, part)
            z = H * n0 + mix(A, u)
            z1[plane, rows, :] = z
            if 1 <= plane <= 4:
                cubes = [cube(v) for v in u]
                q1[plane, rows, :] = n0 - 5.0 * z - (H * cube(n0) + mix(A, cubes))
                d2[plane, rows, :] = mix(B, u)
                if 2 <= plane <= 3:
                    q2[plane, rows, :] = mix(B, cubes)
    for plane in range(1, 5):
        for part in range(4):
            rows = slice(32 * part, 32 * part + 32)
            n1 = sub(q1, plane, part) + fine_sum(z1, plane, part)
            z = H * n1 + sub(d2, plane, part)
            z2[plane, rows, :] = z
            if 2 <= plane <= 3:
                if out1 is not None:
                    out1[first1 + plane - 2, rows, :] = n1
                q2[plane, rows, :] = n1 - 5.0 * z - (H * cube(n1) + sub(q2, plane, part))
    for plane in range(2, 4):
        for part in range(4):
            rows = slice(32 * part, 32 * part + 32)
            out2[first2 + plane - 2, rows, :] = sub(q2, plane, part) + fine_sum(z2, plane, part)


def when(cond, body):
    if cond is None:
        body()
    else:
        pl.when(cond)(body)


class Group:
    def __init__(self, copies, sends=None, receives=None, far=None):
        self.copies, self.sends, self.receives, self.far = copies, sends, receives, far


def kernel(
    ns, nt,
    init_ref, guess_ref, out_ref,
    raw, g, f, n1, n2, f2, i6,
    z1, z2, q1, q2, d2,
    ic, sa, sb, w, v, va, c1, c2, s, t1, t2, halves,
    ssem, rsem, lsem, answer,
):
    t = lax.axis_index("tm")
    c = lax.axis_index("space")
    even = lax.rem(t, 2) == 0
    odd = jnp.logical_not(even)
    low = t < 2
    high = t >= 2
    opposite = lax.rem(t + 2, nt)

    loads = [
        pltpu.make_async_copy(guess_ref.at[0], raw.at[pl.ds(0, 2)], lsem.at[0]),
        pltpu.make_async_copy(init_ref, raw.at[pl.ds(2, 2)], lsem.at[1]),
    ]
    for load in loads:
        load.start()

    def wraps(by):
        return (c + by >= ns) if by > 0 else (c + by < 0)

    def at(by, row=None):
        return (t if row is None else row, lax.rem(c + by + ns, ns))

    up = (jnp.minimum(t + 1, nt - 1), c)
    down = (jnp.maximum(t - 1, 0), c)

    barrier = pltpu.get_barrier_semaphore()
    expected, answers, replies = 0, [0, 0], []

    def signal(semaphore, device):
        pl.semaphore_signal(semaphore, inc=1, device_id=device, device_id_type=MESH)

    def link(sends, receives, source):
        nonlocal expected
        when(receives, lambda: signal(barrier, source))
        expected = expected + (1 if sends is None else jnp.where(sends, 1, 0))

    def far(kind, early, to_late, late, to_early):
        nonlocal expected
        pl.when(early)(lambda: signal(barrier, to_late))
        expected = expected + jnp.where(late, 1, 0)
        answers[kind] = answers[kind] + jnp.where(early, 1, 0)
        replies.append((kind, late, to_early))

    both = [sign * by for by in range(1, REACH + 1) for sign in (1, -1)]
    link(even, odd, down)
    link(odd, even, up)
    far(1, t == 1, up, t == 2, down)
    for by in both:
        if abs(by) <= DEEP:
            link(high | ~wraps(by), high | ~wraps(-by), at(-by))
            link(high & wraps(by), low & wraps(-by), at(-by, opposite))
            far(1, (t == 1) & wraps(by), at(by, 2), (t == 2) & wraps(-by), at(-by, 1))
        else:
            sender = (even if by > 0 else odd) & high
            link(sender, sender, at(-by))
        if -DEEP <= by < 0:
            far(0, low & wraps(by), at(by), low & wraps(-by), at(-by))

    for load in loads:
        load.wait()
    packed = permuted(jnp.concatenate([raw[k] for k in range(4)], axis=0), perm_matrix(True))
    halves[0] = packed[:, :128]
    halves[1] = packed[:, 128:]
    for plane in range(2):
        for row in range(2):
            for col in range(2):
                part = slice(64 * row + 32 * col, 64 * row + 32 * col + 32)
                g[2 + plane, part, :] = halves[col, pl.ds(64 * plane + row, 32, stride=2), :]
                i6[2 + plane, part, :] = halves[col, pl.ds(128 + 64 * plane + row, 32, stride=2), :]
    own = restricted(i6, 2)
    ic[REACH] = own

    @pl.when(t == 0)
    def _():
        f[2:4] = i6[2:4]
        f2[2:4] = i6[2:4]
        for j in range(REACH - DEEP):
            ic[j] = own

    @pl.when(t == 1)
    def _():
        for j in range(REACH + DEEP + 1, 2 * REACH + 1):
            ic[j] = own

    pl.semaphore_wait(barrier, expected)
    for kind, late, to_early in replies:
        pl.when(late)(functools.partial(signal, answer.at[kind], to_early))

    ids = iter(range(200))
    launched, arrived = [], []

    def message(src, dst, device):
        number = next(ids)
        return pltpu.make_async_remote_copy(
            src_ref=src, dst_ref=dst, send_sem=ssem.at[number], recv_sem=rsem.at[number],
            device_id=device, device_id_type=MESH,
        )

    def launch(*groups):
        for group in groups:
            launched.append(group)

            def body(group=group):
                for copy in group.copies:
                    copy.start()

            when(group.sends, body)

    def arrive(*groups):
        for group in groups:
            arrived.append(group)

            def body(group=group):
                for copy in group.copies:
                    copy.wait_recv()

            when(group.receives, body)

    def drain(groups):
        for group in groups:

            def body(group=group):
                for copy in group.copies:
                    copy.wait_send()

            when(group.sends, body)

    def slab(ref, side=0):
        return ref.at[pl.ds(2 + 2 * side, 2)]

    def halo(ref, sends=None, receives=None):
        return Group([message(slab(ref), slab(ref, -1), at(1)), message(slab(ref), slab(ref, 1), at(-1))], sends, receives)

    def spread(ref, middle, reaches, sends=None):
        out = []
        for by in reaches:
            out.append(message(ref.at[middle], ref.at[middle - by], at(by)))
        return Group(out, sends, sends)

    def chunk(ref, k, side=0):
        return ref.at[2 + k // 2 + 2 * side, pl.ds(64 * (k % 2), 64)]

    def crossing(src, dst):
        return [Group([message(chunk(src, k), chunk(dst, k), up)], t == 1, t == 2) for k in range(4)]

    def chunked_halo(ref):
        return [
            [
                Group([message(chunk(ref, k), chunk(ref, k, -by), at(by))], (t == 2) & ~wraps(by), (t == 2) & ~wraps(-by))
                for by in (1, -1)
            ]
            for k in range(4)
        ]

    def around(src, dst):
        return [
            Group([message(slab(src), slab(dst, -by), at(by, 2))], (t == 1) & wraps(by), (t == 2) & wraps(-by))
            for by in (1, -1)
        ]

    def sides(src, dst):
        return Group([message(slab(src, k), slab(dst, k), up) for k in (-1, 1)], even, odd)

    g_cross = crossing(g, f)
    g_halo = [
        Group([message(slab(g), slab(g, -1), at(1))]),
        Group([message(slab(g), slab(g, 1), at(-1))], high | ~wraps(-1), None, low & wraps(-1)),
    ]
    g_core = Group([message(slab(g), slab(f), up)], even, odd)
    g_sides = sides(g, f)
    i_halo = []
    for by in (1, -1):
        row = jnp.where(wraps(by), 0, t)
        copy = message(slab(i6), slab(f, -by), at(by, row))
        i_halo.append(Group([copy], (t == 0) & ~wraps(by) | (t == 2) & wraps(by), t == 0))
    f_halo = chunked_halo(f)
    f_around = around(g, f)
    ic_halo = []
    for by in both:
        sender = even if by > 0 else odd
        if abs(by) > DEEP:
            ic_halo.append(Group([message(ic.at[REACH], ic.at[REACH - by], at(by))], sender & high, sender & high))
            continue
        ic_halo.append(Group([message(ic.at[REACH], ic.at[REACH - by], at(by))], sender & (high | ~wraps(by)), sender & (high | ~wraps(-by))))
        copy = message(ic.at[REACH], ic.at[REACH - by], at(by, opposite))
        ic_halo.append(Group([copy], sender & high & wraps(by), sender & low & wraps(-by)))
    ic_swap = [
        Group([message(ic.at[pl.ds(0, REACH)], ic.at[pl.ds(0, REACH)], up)], even, odd),
        Group([message(ic.at[pl.ds(REACH + 1, REACH)], ic.at[pl.ds(REACH + 1, REACH)], down)], odd, even),
    ]
    v_halo, v0_odd, v0_two = [], [], []
    for by in both[:10]:
        nodes, sums = (v.at[DEEP, pl.ds(1, 2)], v.at[DEEP - by, pl.ds(1, 2)]), (va, v.at[DEEP - by, 1])
        starts = (v.at[DEEP, 0], v.at[DEEP - by, 0])
        far = abs(by)
        if far <= 2:
            v_halo.append(Group([message(*nodes, at(by))]))
            v0_odd.append(Group([message(*starts, at(by))], odd, odd))
        elif far < DEEP:
            v_halo.append(Group([message(*nodes, at(by))], even, even))
        if far == 3:
            v_halo.append(Group([message(*sums, at(by))], odd, odd))
        if far < DEEP:
            v0_two.append(Group([message(*starts, at(by))], t == 2, t == 2))
        else:
            v_halo.append(Group([message(*sums, at(by))], even, even))
    n1_halo = halo(n1)
    n2_halo = halo(n2)
    n2_cross = crossing(n2, f2)
    n2_core = Group([message(slab(n2), slab(f2), up)], even, odd)
    n2_sides = sides(n2, f2)
    f2_halo = chunked_halo(f2)
    f2_around = around(n2, f2)
    s_core = Group([message(t2.at[pl.ds(2, 7)], s.at[pl.ds(2, 7)], up)], even, odd)
    s_cross = Group([message(t2.at[DEEP], s.at[DEEP], up)], t == 1, t == 2)
    s_wrapped, s_spread = [], []
    for by in both[:10]:
        number = next(ids)
        for groups, src, sends in ((s_wrapped, t2, (t == 1) & wraps(by)), (s_spread, s, (t == 2) & ~wraps(by))):
            copy = pltpu.make_async_remote_copy(
                src_ref=src.at[DEEP], dst_ref=s.at[DEEP - by], send_sem=ssem.at[number], recv_sem=rsem.at[number],
                device_id=at(by, 2), device_id_type=MESH,
            )
            groups.append(Group([copy], sends, t == 2))

    launch(*ic_halo)
    launch(*g_halo)
    launch(g_core)
    launch(*i_halo)

    pl.when(answers[0] > 0)(lambda: pl.semaphore_wait(answer.at[0], answers[0]))
    launch(*(Group(x.copies, x.far) for x in (*ic_halo, *g_halo) if x.far is not None))

    arrive(g_core)

    @pl.when(odd)
    def _():
        v[DEEP, 0] = restricted(f, 2)

    launch(*v0_odd)

    edge = (c < DEEP) | (c >= ns - DEEP)

    def cross(here):
        pl.when((t == 1) & here)(lambda: pl.semaphore_wait(answer.at[1], answers[1]))
        launch(*(Group(x.copies, x.sends & here) for x in (*g_cross, *f_around)))

    cross(edge)

    arrive(*ic_halo)
    launch(*ic_swap)
    arrive(*ic_swap)

    for j in range(2 * REACH + 1):
        sa[j] = ic[j]

    sb[0] = own
    sb[2 * REACH] = own

    def two_steps(_, carry):
        for j in range(1, 2 * REACH):
            sb[j] = euler(sa[j - 1], sa[j], sa[j + 1])
        for j in range(2, 2 * REACH - 1):
            sa[j] = euler(sb[j - 1], sb[j], sb[j + 1])
        return carry

    lax.fori_loop(0, t, two_steps, 0)
    for j in range(REACH - 2, REACH + 3):
        sb[j] = euler(sa[j - 1], sa[j], sa[j + 1])
    for j in range(3):
        k = REACH - 1 + j
        w[0, j] = sa[k]
        w[1, j] = sb[k]
        w[2, j] = euler(sb[k - 1], sb[k], sb[k + 1])

    arrive(*g_halo)
    launch(g_sides)

    arrive(g_sides, *i_halo)
    for crossed, passed in zip(g_cross, f_halo):
        arrive(crossed)
        launch(*passed)

    @pl.when(t == 2)
    def _():
        v[DEEP, 0] = restricted(f, 2)

    @pl.when(t == 0)
    def _():
        for j in range(2 * DEEP + 1):
            v[j, 0] = ic[REACH - DEEP + j]

    launch(*v0_two)
    for passed in f_halo:
        arrive(*passed)
    arrive(*f_around)

    old = [restricted(g, 2 * j) for j in range(3)]
    shifts = [[w[m, j] - old[j] for j in range(3)] for m in range(3)]
    fine_sweep((g, g, g), shifts, f, z1, z2, q1, q2, d2, n1, 2, n2, 2)

    first = list(launched)
    v[DEEP, 1] = restricted(n1, 2)
    v[DEEP, 2] = restricted(n2, 2)
    va[...] = mix(A, [v[DEEP, m] for m in range(3)])
    launch(*v_halo)
    launch(n2_core)
    cross(~edge)

    n_halo = [n1_halo, n2_halo]
    launch(*(Group(x.copies, high & edge) for x in n_halo))
    arrive(s_cross)
    launch(*s_spread)
    launch(*(Group(x.copies, high & ~edge) for x in n_halo))
    drain(first)
    arrive(*v0_odd, *v0_two, *v_halo)
    launch(*(Group(x.copies, low) for x in n_halo))

    def forcing(weights, out, j, sums=()):
        z = [v[k, 1] if k in sums else mix(weights, [v[k, m] for m in range(3)]) for k in (j - 1, j, j + 1)]
        cubes = mix(weights, [cube(v[j, m]) for m in range(3)])
        out[j] = 0.25 * coarse_sum(*z) - 0.5 * z[1] - cubes

    def forcings(reach):
        for j in range(DEEP - reach, DEEP + reach + 1):
            forcing(A, c1, j, (DEEP - reach - 1, DEEP + reach + 1))
            if abs(j - DEEP) < reach:
                forcing(B, c2, j)

    def chain(reach):
        for j in range(DEEP - reach, DEEP + reach + 1):
            t1[j] = euler(s[j - 1], s[j], s[j + 1]) + c1[j]
        for j in range(DEEP - reach + 1, DEEP + reach):
            t2[j] = euler(t1[j - 1], t1[j], t1[j + 1]) + c2[j]

    when(even, lambda: forcings(4))
    when(odd, lambda: forcings(2))

    @pl.when(t == 0)
    def _():
        f2[0:2] = f[0:2]
        f2[4:6] = f[4:6]
        for j in range(2 * DEEP + 1):
            s[j] = ic[REACH - DEEP + j]

    for crossed, passed in zip(n2_cross, f2_halo):
        arrive(crossed)
        launch(*passed)

    arrive(*s_spread)

    when(even, lambda: chain(4))
    launch(s_core)
    arrive(s_core)
    when(odd, lambda: chain(2))
    launch(s_cross)
    launch(*s_wrapped)
    launch(*n2_cross, *f2_around)

    arrive(n2_halo)
    launch(n2_sides)

    arrive(n1_halo, n2_core, n2_sides, *f2_around)
    for passed in f2_halo:
        arrive(*passed)

    shifts = []
    for m, level in enumerate((s, t1, t2)):
        shifts.append([level[DEEP - 1 + j] - v[DEEP - 1 + j, m] for j in range(3)])
    fine_sweep((f, n1, n2), shifts, f2, z1, z2, q1, q2, d2, None, 0, out_ref, 0)

    drain(launched[len(first) :])


def interleave(x_ref, out_ref, halves):
    for plane in range(2):
        for row in range(2):
            for col in range(2):
                halves[col, pl.ds(64 * plane + row, 32, stride=2), :] = sub(x_ref, plane, 2 * row + col)
    wide = permuted(jnp.concatenate([halves[0], halves[1]], axis=1), perm_matrix(False))
    out_ref[0, 0] = wide[:64]
    out_ref[0, 1] = wide[64:]


def solution(mesh):
    ns, nt = mesh.shape["space"], mesh.shape["tm"]
    vmem = pl.BlockSpec(memory_space=pltpu.VMEM)

    def local(initial, guess):
        slab6 = pltpu.VMEM((6, 128, 128), jnp.float32)

        def planes(*lead):
            return pltpu.VMEM((*lead, 32, 128), jnp.float32)

        last = pl.pallas_call(
            functools.partial(kernel, ns, nt),
            out_shape=pltpu.VMEM((2, 128, 128), jnp.float32),
            in_specs=[pl.BlockSpec(memory_space=pltpu.HBM)] * 2,
            out_specs=vmem,
            scratch_shapes=[pltpu.VMEM((4, 64, 256), jnp.float32)]
            + [slab6] * 11
            + [planes(2 * REACH + 1)] * 3
            + [planes(3, 3), planes(2 * DEEP + 1, 3), planes()]
            + [planes(2 * DEEP + 1)] * 5
            + [pltpu.VMEM((2, 256, 128), jnp.float32)]
            + [pltpu.SemaphoreType.DMA((160,))] * 2
            + [pltpu.SemaphoreType.DMA((2,)), pltpu.SemaphoreType.REGULAR((2,))],
            compiler_params=pltpu.CompilerParams(
                collective_id=0, has_side_effects=True, vmem_limit_bytes=32 << 20
            ),
            name="pfasst",
        )(*(pltpu.with_memory_space_constraint(x, pltpu.HBM) for x in (initial, guess)))
        return pl.pallas_call(
            interleave,
            out_shape=jax.ShapeDtypeStruct(guess.shape, jnp.float32),
            in_specs=[vmem],
            out_specs=vmem,
            scratch_shapes=[pltpu.VMEM((2, 128, 128), jnp.float32)],
            compiler_params=pltpu.CompilerParams(vmem_limit_bytes=32 << 20),
            name="interleave",
        )(last)

    return jax.shard_map(
        local,
        mesh=mesh,
        in_specs=(P("space", None, None), P("tm", "space", None, None)),
        out_specs=P("tm", "space", None, None),
        check_vma=False,
    )
```

time: 66.9 us -> 55.8 us (0.83)
  the two profiles are of different devices: /device:TPU:257 before, /device:TPU:1 now
where the time goes in v2:
time: 55.8 us; the launch traced here: 55.6 us
  Pallas kernels  55.6 us (100%)
    pallas_call x1, Pallas kernels, local(): pl.pallas_call(functools.partial(kernel, ns, nt), out_shape=pltpu.VMEM((2...  54.7 us

profile of v2, /device:TPU:1, one launch (start us, length us, event | category | flops | bytes accessed | tf_op | source)
XLA Modules:
  0.0 55.6 jit_solution(11663512250243532765)
XLA Ops:
  0.0 54.7 %pfasst.1.x_ref = f32[2,128,128]{2,1,0:T(8,128)S(1)} custom-call(f32[2,64,256]{2,1,0:T(8,128)} %init_ref.1, f32[1,2,64,256]{3,2,1,0:T(8,128)} %guess_ref.1), custom_call_target="tpu_custom_call" | custom-call | tf_op jit(solution)/shard_map/pfasst/pallas_call | solution.py:531
  54.7 0.9 %interleave.1 = f32[1,2,64,256]{3,2,1,0:T(8,128)} custom-call(f32[2,128,128]{2,1,0:T(8,128)S(1)} %pfasst.1.x_ref), custom_call_target="tpu_custom_call" | custom-call | tf_op jit(solution)/shard_map/interleave/pallas_call | solution.py:549

commit v3 on v2

v3 whole, which is shorter than its diff:
```python
import functools

import jax
import jax.numpy as jnp
from jax import lax
from jax.experimental import pallas as pl
from jax.experimental.pallas import tpu as pltpu
from jax.sharding import PartitionSpec as P

MESH = pl.DeviceIdType.MESH
DT, H = 0.24, 0.12
A = (DT * 5.0 / 24.0 - H, DT / 3.0, -DT / 24.0)
B = (-DT / 24.0, DT / 3.0 - H, DT * 5.0 / 24.0)
REACH = 9
DEEP = 5


def split(x):
    high = x.astype(jnp.bfloat16)
    rest = x - high.astype(jnp.float32)
    mid = rest.astype(jnp.bfloat16)
    low = (rest - mid.astype(jnp.float32)).astype(jnp.bfloat16)
    return jnp.concatenate([high, mid, low], axis=0)


def permuted(x, perm):
    rows = x.shape[0]
    out = jnp.dot(split(x), perm, preferred_element_type=jnp.float32)
    return out[:rows] + (out[rows : 2 * rows] + out[2 * rows :])


def perm_matrix(to_parity):
    i = lax.broadcasted_iota(jnp.int32, (256, 256), 0)
    j = lax.broadcasted_iota(jnp.int32, (256, 256), 1)
    wide, packed = (i, j) if to_parity else (j, i)
    lane = jnp.where(packed < 128, 2 * packed, 2 * packed - 255)
    return jnp.where(wide == lane, 1.0, 0.0).astype(jnp.bfloat16)


def lane_roll(x, by):
    return pltpu.roll(x, by % 128, 1)


def row_roll(x, by):
    return pltpu.roll(x, by % 32, 0)


def coarse_sum(below, x, above):
    total = below + above
    total = total + lane_roll(x, 1) + lane_roll(x, -1)
    return total + row_roll(x, 1) + row_roll(x, -1)


def euler(below, x, above):
    return 0.25 * H * coarse_sum(below, x, above) + x * ((1.0 - 0.5 * H) - H * (x * x))


def cube(x):
    return x * x * x


def mix(weights, values):
    return weights[0] * values[0] + weights[1] * values[1] + weights[2] * values[2]


def sub(ref, plane, part):
    return ref[plane, 32 * part : 32 * part + 32, :]


def restricted(ref, first):
    total = None
    for plane in (first, first + 1):
        for part in range(4):
            piece = sub(ref, plane, part)
            total = piece if total is None else total + piece
    return 0.125 * total


def fine_sum(ref, plane, part):
    row, col = part // 2, part % 2
    beside = sub(ref, plane, row * 2 + 1 - col)
    over = sub(ref, plane, (1 - row) * 2 + col)
    total = sub(ref, plane - 1, part) + sub(ref, plane + 1, part)
    total = total + beside + lane_roll(beside, 1 if col == 0 else -1)
    return total + over + row_roll(over, 1 if row == 0 else -1)


def fine_sweep(nodes, shifts, start, z1, z2, q1, q2, d2, out1, first1, out2, first2):
    for plane in range(6):
        for part in range(4):
            rows = slice(32 * part, 32 * part + 32)
            u = [sub(nodes[m], plane, part) + shifts[m][plane // 2] for m in range(3)]
            n0 = sub(start, plane, part)
            z = H * n0 + mix(A, u)
            z1[plane, rows, :] = z
            if 1 <= plane <= 4:
                cubes = [cube(v) for v in u]
                q1[plane, rows, :] = n0 - 5.0 * z - (H * cube(n0) + mix(A, cubes))
                d2[plane, rows, :] = mix(B, u)
                if 2 <= plane <= 3:
                    q2[plane, rows, :] = mix(B, cubes)
    for plane in range(1, 5):
        for part in range(4):
            rows = slice(32 * part, 32 * part + 32)
            n1 = sub(q1, plane, part) + fine_sum(z1, plane, part)
            z = H * n1 + sub(d2, plane, part)
            z2[plane, rows, :] = z
            if 2 <= plane <= 3:
                if out1 is not None:
                    out1[first1 + plane - 2, rows, :] = n1
                q2[plane, rows, :] = n1 - 5.0 * z - (H * cube(n1) + sub(q2, plane, part))
    for plane in range(2, 4):
        for part in range(4):
            rows = slice(32 * part, 32 * part + 32)
            out2[first2 + plane - 2, rows, :] = sub(q2, plane, part) + fine_sum(z2, plane, part)


IC, SWAP, GUESS, CORE, SIDES, STARTS, NODES, N1, N2, CORE2, SIDES2, CROSS, SPREAD, PAIR, A_CHUNK, B_CHUNK = range(16)
CHUNKS = 4


def kernel(
    ns, nt,
    init_ref, guess_ref, out_ref,
    raw, g, f, n1, n2, f2, i6,
    z1, z2, q1, q2, d2,
    ic, sa, sb, w, v, va, c1, c2, s, t1, t2, halves,
    ssem, rsem, lsem, answer, passed,
):
    t = lax.axis_index("tm")
    c = lax.axis_index("space")
    even = lax.rem(t, 2) == 0
    odd = lax.rem(t, 2) == 1
    low, high = t < 2, t >= 2
    opposite = lax.rem(t + 2, nt)
    middle = (c >= REACH) & (c < ns - REACH)
    outer = (c < REACH) | (c >= ns - REACH)
    edge = (c < DEEP) | (c >= ns - DEEP)
    inland = (c >= DEEP) & (c < ns - DEEP)

    loads = [
        pltpu.make_async_copy(guess_ref.at[0], raw.at[pl.ds(0, 2)], lsem.at[0]),
        pltpu.make_async_copy(init_ref, raw.at[pl.ds(2, 2)], lsem.at[1]),
    ]
    for load in loads:
        load.start()

    def wraps(by):
        return (c + by >= ns) if by > 0 else (c + by < 0)

    def at(by, row=None):
        return (t if row is None else row, lax.rem(c + by + ns, ns))

    up = (jnp.minimum(t + 1, nt - 1), c)
    down = (jnp.maximum(t - 1, 0), c)

    barrier = pltpu.get_barrier_semaphore()
    row = jnp.minimum(t, 2)

    def signal(semaphore, device):
        pl.semaphore_signal(semaphore, inc=1, device_id=device, device_id_type=MESH)

    near = [sign * by for by in range(1, DEEP + 1) for sign in (1, -1)]

    @pl.when(edge)
    def _():
        for by in near:

            @pl.when(wraps(by))
            def _(by=by):
                signal(barrier, at(by, row))
                pl.when(low)(lambda: signal(barrier, at(by, 2)))
                pl.when(t == 1)(lambda: signal(barrier, at(by, 3)))

    pl.when(even)(lambda: signal(barrier, up))
    pl.when(odd)(lambda: signal(barrier, down))
    pl.when(t == 1)(lambda: signal(barrier, (3, c)))
    for by in near:
        pl.when(jnp.logical_not(wraps(by)))(lambda by=by: signal(barrier, at(by, row)))

    @pl.when(high & even)
    def _():
        for by in range(DEEP + 1, REACH + 1):
            signal(barrier, at(-by))

    @pl.when(high & odd)
    def _():
        for by in range(DEEP + 1, REACH + 1):
            signal(barrier, at(by, 2))

    around = 0
    for by in near:
        around = around + jnp.where(wraps(by), 1, 0)
    count = len(near)
    expected = jnp.where(low, count + 1, jnp.where(t == 2, 2 * count + 2 * (REACH - DEEP) + 1 + 2 * around, 2 + around))

    for load in loads:
        load.wait()
    packed = permuted(jnp.concatenate([raw[k] for k in range(4)], axis=0), perm_matrix(True))
    halves[0] = packed[:, :128]
    halves[1] = packed[:, 128:]
    for plane in range(2):
        for row in range(2):
            for col in range(2):
                part = slice(64 * row + 32 * col, 64 * row + 32 * col + 32)
                g[2 + plane, part, :] = halves[col, pl.ds(64 * plane + row, 32, stride=2), :]
                i6[2 + plane, part, :] = halves[col, pl.ds(128 + 64 * plane + row, 32, stride=2), :]
    own = restricted(i6, 2)
    ic[REACH] = own

    @pl.when(t == 0)
    def _():
        f[2:4] = i6[2:4]
        f2[2:4] = i6[2:4]
        for j in range(REACH - DEEP):
            ic[j] = own

    @pl.when(t == 1)
    def _():
        for j in range(REACH + DEEP + 1, 2 * REACH + 1):
            ic[j] = own

    pl.semaphore_wait(barrier, expected)

    @pl.when(t == 3)
    def _():
        signal(answer, (1, c))

        @pl.when(edge)
        def _():
            for by in near:
                pl.when(wraps(by))(lambda by=by: signal(answer, at(by, 1)))

        pl.semaphore_wait(passed, 1)

    @pl.when(t == 2)
    def _():
        signal(passed, up)

    ids = iter(range(200))
    launched = []

    def message(src, dst, number, device):
        return pltpu.make_async_remote_copy(
            src_ref=src, dst_ref=dst, send_sem=ssem.at[next(ids)], recv_sem=rsem.at[number],
            device_id=device, device_id_type=MESH,
        )

    def each(sends, items, act):
        if all(wrapped is None for _, wrapped in items):

            @pl.when(sends)
            def _():
                for copy, _ in items:
                    act(copy)

            return
        inner = [copy for copy, wrapped in items if wrapped is None or not wrapped[1]]
        if inner:

            @pl.when(sends & middle)
            def _():
                for copy in inner:
                    act(copy)

        @pl.when(sends & outer)
        def _():
            for copy, wrapped in items:
                if wrapped is None:
                    act(copy)
                elif wrapped[1]:
                    pl.when(wraps(wrapped[0]))(functools.partial(act, copy))
                else:
                    pl.when(jnp.logical_not(wraps(wrapped[0])))(functools.partial(act, copy))

    def launch(sends, items):
        launched.append((sends, items))
        each(sends, items, lambda copy: copy.start())

    def drain(groups):
        for sends, items in groups:
            each(sends, items, lambda copy: copy.wait_send())

    def landed(ref, number):
        pltpu.make_async_remote_copy(
            src_ref=ref, dst_ref=ref, send_sem=ssem.at[0], recv_sem=rsem.at[number],
            device_id=up, device_id_type=MESH,
        ).wait_recv()

    always = t >= 0

    def slab(ref, side=0):
        return ref.at[pl.ds(2 + 2 * side, 2)]

    def slabs(ref):
        return ref.at[pl.ds(0, 4)]

    def halo(ref, number):
        return [(message(slab(ref), slab(ref, -by), number, at(by)), None) for by in (1, -1)]

    def chunk(ref, k, side=0):
        return ref.at[2 + k // 2 + 2 * side, pl.ds(64 * (k % 2), 64)]

    def crossing(src, dst, number, sides):
        out = [(message(chunk(src, k), chunk(dst, k), number + 2 * k, up), None) for k in range(CHUNKS)]
        return out + [(message(slab(src), slab(dst, -by), sides, at(by, 2)), (by, True)) for by in (1, -1)]

    def forward(ref, k, number):
        return [(message(chunk(ref, k), chunk(ref, k, -by), number, at(by)), (by, False)) for by in (1, -1)]

    def sides(src, dst, number):
        return [(message(slab(src, k), slab(dst, k), number, up), None) for k in (-1, 1)]

    def plane(by, device, wrapped):
        return (message(ic.at[REACH], ic.at[REACH - by], IC, device), wrapped)

    for sender, sign in ((even, 1), (odd, -1)):
        offsets = [sign * by for by in range(1, REACH + 1)]
        launch(sender & low, [plane(by, at(by), (by, False)) for by in offsets[:DEEP]])
        launch(
            sender & high,
            [plane(by, at(by), None) for by in offsets]
            + [plane(by, at(by, opposite), (by, True)) for by in offsets[:DEEP]],
        )
    launch(always, halo(g, GUESS))
    launch(even, [(message(slab(g), slab(f), CORE, up), None)])
    launch(t == 0, [(message(slab(i6), slab(f, -by), SIDES, at(by)), (by, False)) for by in (1, -1)])
    launch(t == 2, [(message(slab(i6), slab(f, -by), SIDES, at(by, 0)), (by, True)) for by in (1, -1)])

    def start_planes(reach):
        return [
            (message(v.at[DEEP, 0], v.at[DEEP - sign * by, 0], STARTS, at(sign * by)), None)
            for by in range(1, reach + 1) for sign in (1, -1)
        ]

    @pl.when(odd)
    def _():
        landed(slab(f), CORE)
        v[DEEP, 0] = restricted(f, 2)

    launch(odd, start_planes(2))

    answers = 1 + around
    crossed = crossing(g, f, A_CHUNK, SIDES)

    @pl.when((t == 1) & edge)
    def _():
        pl.semaphore_wait(answer, answers)

    launch((t == 1) & edge, crossed)

    @pl.when(even)
    def _():
        pl.when(low)(lambda: landed(ic.at[pl.ds(REACH - DEEP, DEEP)], IC))
        pl.when(high)(lambda: landed(ic.at[pl.ds(0, REACH)], IC))

    @pl.when(odd)
    def _():
        pl.when(low)(lambda: landed(ic.at[pl.ds(REACH + 1, DEEP)], IC))
        pl.when(high)(lambda: landed(ic.at[pl.ds(REACH + 1, REACH)], IC))

    left, right = ic.at[pl.ds(0, REACH)], ic.at[pl.ds(REACH + 1, REACH)]
    launch(even, [(message(left, left, SWAP, up), None)])
    launch(odd, [(message(right, right, SWAP, down), None)])
    pl.when(even)(lambda: landed(right, SWAP))
    pl.when(odd)(lambda: landed(left, SWAP))

    for j in range(2 * REACH + 1):
        sa[j] = ic[j]

    sb[0] = own
    sb[2 * REACH] = own

    def two_steps(_, carry):
        for j in range(1, 2 * REACH):
            sb[j] = euler(sa[j - 1], sa[j], sa[j + 1])
        for j in range(2, 2 * REACH - 1):
            sa[j] = euler(sb[j - 1], sb[j], sb[j + 1])
        return carry

    lax.fori_loop(0, t, two_steps, 0)
    for j in range(REACH - 2, REACH + 3):
        sb[j] = euler(sa[j - 1], sa[j], sa[j + 1])
    for j in range(3):
        k = REACH - 1 + j
        w[0, j] = sa[k]
        w[1, j] = sb[k]
        w[2, j] = euler(sb[k - 1], sb[k], sb[k + 1])

    landed(slabs(g), GUESS)
    launch(even, sides(g, f, SIDES))

    for k in range(CHUNKS):
        pl.when(t == 2)(lambda k=k: landed(chunk(f, k), A_CHUNK + 2 * k))
        launch(t == 2, forward(f, k, SIDES))

    @pl.when(t == 2)
    def _():
        v[DEEP, 0] = restricted(f, 2)

    @pl.when(t == 0)
    def _():
        for j in range(2 * DEEP + 1):
            v[j, 0] = ic[REACH - DEEP + j]

    launch(t == 2, start_planes(4))
    landed(slabs(f), SIDES)

    old = [restricted(g, 2 * j) for j in range(3)]
    shifts = [[w[m, j] - old[j] for j in range(3)] for m in range(3)]
    fine_sweep((g, g, g), shifts, f, z1, z2, q1, q2, d2, n1, 2, n2, 2)

    first = list(launched)
    v[DEEP, 1] = restricted(n1, 2)
    v[DEEP, 2] = restricted(n2, 2)
    va[...] = mix(A, [v[DEEP, m] for m in range(3)])

    def node_planes(by):
        return (message(v.at[DEEP, pl.ds(1, 2)], v.at[DEEP - by, pl.ds(1, 2)], NODES, at(by)), None)

    def sum_plane(by):
        return (message(va, v.at[DEEP - by, 1], NODES, at(by)), None)

    launch(even, [node_planes(by) for by in near[:8]] + [sum_plane(by) for by in near[8:]])
    launch(odd, [node_planes(by) for by in near[:4]] + [sum_plane(by) for by in near[4:6]])
    launch(even, [(message(slab(n2), slab(f2), CORE2, up), None)])

    @pl.when((t == 1) & inland)
    def _():
        pl.semaphore_wait(answer, answers)

    launch((t == 1) & inland, crossed)

    n_halo = halo(n2, N2) + halo(n1, N1)
    launch(high & edge, n_halo)
    pl.when(t == 2)(lambda: landed(s.at[DEEP], CROSS))
    launch(
        t == 2,
        [(message(s.at[DEEP], s.at[DEEP - by], SPREAD, at(by)), (by, False)) for by in near],
    )
    launch(high & inland, n_halo)
    drain(first)

    @pl.when(even)
    def _():
        pl.when(high)(lambda: landed(v.at[pl.ds(0, 8), 0], STARTS))
        landed(v.at[pl.ds(0, 6)], NODES)

    @pl.when(odd)
    def _():
        landed(v.at[pl.ds(0, 4), 0], STARTS)
        landed(v.at[pl.ds(0, 5), pl.ds(1, 2)], NODES)

    launch(low, n_halo)

    for k in range(CHUNKS):
        pl.when(t == 2)(lambda k=k: landed(chunk(f2, k), B_CHUNK + 2 * k))
        launch(t == 2, forward(f2, k, SIDES2))

    def forcing(weights, out, j, sums=()):
        z = [v[k, 1] if k in sums else mix(weights, [v[k, m] for m in range(3)]) for k in (j - 1, j, j + 1)]
        cubes = mix(weights, [cube(v[j, m]) for m in range(3)])
        out[j] = 0.25 * coarse_sum(*z) - 0.5 * z[1] - cubes

    def forcings(reach):
        for j in range(DEEP - reach, DEEP + reach + 1):
            forcing(A, c1, j, (DEEP - reach - 1, DEEP + reach + 1))
            if abs(j - DEEP) < reach:
                forcing(B, c2, j)

    def chain(reach):
        for j in range(DEEP - reach, DEEP + reach + 1):
            t1[j] = euler(s[j - 1], s[j], s[j + 1]) + c1[j]
        for j in range(DEEP - reach + 1, DEEP + reach):
            t2[j] = euler(t1[j - 1], t1[j], t1[j + 1]) + c2[j]

    pl.when(even)(lambda: forcings(4))
    pl.when(odd)(lambda: forcings(2))

    @pl.when(t == 0)
    def _():
        f2[0:2] = f[0:2]
        f2[4:6] = f[4:6]
        for j in range(2 * DEEP + 1):
            s[j] = ic[REACH - DEEP + j]

    pl.when(t == 2)(lambda: landed(s.at[pl.ds(0, 10)], SPREAD))

    pl.when(even)(lambda: chain(4))
    launch(even, [(message(t2.at[pl.ds(2, 7)], s.at[pl.ds(2, 7)], PAIR, up), None)])

    @pl.when(odd)
    def _():
        landed(s.at[pl.ds(2, 7)], PAIR)
        chain(2)

    launch(
        t == 1,
        [(message(t2.at[DEEP], s.at[DEEP], CROSS, up), None)]
        + [(message(t2.at[DEEP], s.at[DEEP - by], SPREAD, at(by, 2)), (by, True)) for by in near],
    )
    crossed = crossing(n2, f2, B_CHUNK, SIDES2)
    launch((t == 1) & edge, crossed)

    landed(slabs(n2), N2)
    launch(even, sides(n2, f2, SIDES2))
    landed(slabs(n1), N1)
    launch((t == 1) & inland, crossed)

    pl.when(odd)(lambda: landed(slab(f2), CORE2))
    pl.when(t > 0)(lambda: landed(slabs(f2), SIDES2))

    shifts = []
    for m, level in enumerate((s, t1, t2)):
        shifts.append([level[DEEP - 1 + j] - v[DEEP - 1 + j, m] for j in range(3)])
    fine_sweep((f, n1, n2), shifts, f2, z1, z2, q1, q2, d2, None, 0, out_ref, 0)

    drain(launched[len(first) :])


def interleave(x_ref, out_ref, halves):
    for plane in range(2):
        for row in range(2):
            for col in range(2):
                halves[col, pl.ds(64 * plane + row, 32, stride=2), :] = sub(x_ref, plane, 2 * row + col)
    wide = permuted(jnp.concatenate([halves[0], halves[1]], axis=1), perm_matrix(False))
    out_ref[0, 0] = wide[:64]
    out_ref[0, 1] = wide[64:]


def solution(mesh):
    ns, nt = mesh.shape["space"], mesh.shape["tm"]
    vmem = pl.BlockSpec(memory_space=pltpu.VMEM)

    def local(initial, guess):
        slab6 = pltpu.VMEM((6, 128, 128), jnp.float32)

        def planes(*lead):
            return pltpu.VMEM((*lead, 32, 128), jnp.float32)

        last = pl.pallas_call(
            functools.partial(kernel, ns, nt),
            out_shape=pltpu.VMEM((2, 128, 128), jnp.float32),
            in_specs=[pl.BlockSpec(memory_space=pltpu.HBM)] * 2,
            out_specs=vmem,
            scratch_shapes=[pltpu.VMEM((4, 64, 256), jnp.float32)]
            + [slab6] * 11
            + [planes(2 * REACH + 1)] * 3
            + [planes(3, 3), planes(2 * DEEP + 1, 3), planes()]
            + [planes(2 * DEEP + 1)] * 5
            + [pltpu.VMEM((2, 256, 128), jnp.float32)]
            + [pltpu.SemaphoreType.DMA((160,)), pltpu.SemaphoreType.DMA((24,))]
            + [pltpu.SemaphoreType.DMA((2,)), pltpu.SemaphoreType.REGULAR, pltpu.SemaphoreType.REGULAR],
            compiler_params=pltpu.CompilerParams(
                collective_id=0, has_side_effects=True, vmem_limit_bytes=32 << 20
            ),
            name="pfasst",
        )(*(pltpu.with_memory_space_constraint(x, pltpu.HBM) for x in (initial, guess)))
        return pl.pallas_call(
            interleave,
            out_shape=jax.ShapeDtypeStruct(guess.shape, jnp.float32),
            in_specs=[vmem],
            out_specs=vmem,
            scratch_shapes=[pltpu.VMEM((2, 128, 128), jnp.float32)],
            compiler_params=pltpu.CompilerParams(vmem_limit_bytes=32 << 20),
            name="interleave",
        )(last)

    return jax.shard_map(
        local,
        mesh=mesh,
        in_specs=(P("space", None, None), P("tm", "space", None, None)),
        out_specs=P("tm", "space", None, None),
        check_vma=False,
    )
```

time: 55.8 us -> 53.3 us (0.955)
  the two profiles are of different devices: /device:TPU:1 before, /device:TPU:488 now
where the time goes in v3:
time: 53.3 us; the launch traced here: 53.2 us
  Pallas kernels  53.2 us (100%)
    pallas_call x1, Pallas kernels, local(): pl.pallas_call(functools.partial(kernel, ns, nt), out_shape=pltpu.VMEM((2...  52.3 us

profile of v3, /device:TPU:488, one launch (start us, length us, event | category | flops | bytes accessed | tf_op | source)
XLA Modules:
  0.0 53.2 jit_solution(11213364578080078383)
XLA Ops:
  0.0 52.3 %pfasst.1.x_ref = f32[2,128,128]{2,1,0:T(8,128)S(1)} custom-call(f32[2,64,256]{2,1,0:T(8,128)} %init_ref.1, f32[1,2,64,256]{3,2,1,0:T(8,128)} %guess_ref.1), custom_call_target="tpu_custom_call" | custom-call | tf_op jit(solution)/shard_map/pfasst/pallas_call | solution.py:541
  52.3 0.9 %interleave.1 = f32[1,2,64,256]{3,2,1,0:T(8,128)} custom-call(f32[2,128,128]{2,1,0:T(8,128)S(1)} %pfasst.1.x_ref), custom_call_target="tpu_custom_call" | custom-call | tf_op jit(solution)/shard_map/interleave/pallas_call | solution.py:559

commit v4 on v3

--- a/solution.py
+++ b/solution.py
@@ -136,6 +136,8 @@
     middle = (c >= REACH) & (c < ns - REACH)
     outer = (c < REACH) | (c >= ns - REACH)
     edge = (c < DEEP) | (c >= ns - DEEP)
+    soon = (c < DEEP) | (c >= 3 * ns // 4)
+    later = (c >= DEEP) & (c < 3 * ns // 4)
     inland = (c >= DEEP) & (c < ns - DEEP)
 
     loads = [
@@ -343,11 +345,11 @@
     answers = 1 + around
     crossed = crossing(g, f, A_CHUNK, SIDES)
 
-    @pl.when((t == 1) & edge)
+    @pl.when((t == 1) & soon)
     def _():
         pl.semaphore_wait(answer, answers)
 
-    launch((t == 1) & edge, crossed)
+    launch((t == 1) & soon, crossed)
 
     @pl.when(even)
     def _():
@@ -425,14 +427,18 @@
     launch(odd, [node_planes(by) for by in near[:4]] + [sum_plane(by) for by in near[4:6]])
     launch(even, [(message(slab(n2), slab(f2), CORE2, up), None)])
 
-    @pl.when((t == 1) & inland)
+    @pl.when((t == 1) & later)
     def _():
         pl.semaphore_wait(answer, answers)
 
-    launch((t == 1) & inland, crossed)
+    launch((t == 1) & later, crossed)
 
     n_halo = halo(n2, N2) + halo(n1, N1)
     launch(high & edge, n_halo)
+    n_inner = [(copy, (by, False)) for (copy, _), by in zip(n_halo, (1, -1, 1, -1))]
+    n_around = [(copy, (by, True)) for (copy, _), by in zip(n_halo, (1, -1, 1, -1))]
+    launch(low & edge, n_inner)
+    launch(low & (c == ns - 1), n_around)
     pl.when(t == 2)(lambda: landed(s.at[DEEP], CROSS))
     launch(
         t == 2,
@@ -451,7 +457,9 @@
         landed(v.at[pl.ds(0, 4), 0], STARTS)
         landed(v.at[pl.ds(0, 5), pl.ds(1, 2)], NODES)
 
-    launch(low, n_halo)
+
+    crossed = crossing(n2, f2, B_CHUNK, SIDES2)
+    launch((t == 1) & later, crossed)
 
     for k in range(CHUNKS):
         pl.when(t == 2)(lambda k=k: landed(chunk(f2, k), B_CHUNK + 2 * k))
@@ -499,13 +507,14 @@
         [(message(t2.at[DEEP], s.at[DEEP], CROSS, up), None)]
         + [(message(t2.at[DEEP], s.at[DEEP - by], SPREAD, at(by, 2)), (by, True)) for by in near],
     )
-    crossed = crossing(n2, f2, B_CHUNK, SIDES2)
-    launch((t == 1) & edge, crossed)
+    launch((t == 1) & soon, crossed)
+
+    launch(low & inland, n_halo)
+    launch(low & (c == 0), n_around)
 
     landed(slabs(n2), N2)
     launch(even, sides(n2, f2, SIDES2))
     landed(slabs(n1), N1)
-    launch((t == 1) & inland, crossed)
 
     pl.when(odd)(lambda: landed(slab(f2), CORE2))
     pl.when(t > 0)(lambda: landed(slabs(f2), SIDES2))

time: 53.3 us -> 50.8 us (0.953)
  the two profiles are of different devices: /device:TPU:488 before, /device:TPU:1 now
where the time goes in v4:
time: 50.8 us; the launch traced here: 50.6 us
  Pallas kernels  50.6 us (100%)
    pallas_call x1, Pallas kernels, local(): pl.pallas_call(functools.partial(kernel, ns, nt), out_shape=pltpu.VMEM((2...  49.8 us

profile of v4, /device:TPU:1, one launch (start us, length us, event | category | flops | bytes accessed | tf_op | source)
XLA Modules:
  0.0 50.6 jit_solution(10226432947674184707)
XLA Ops:
  0.0 49.8 %pfasst.1.x_ref = f32[2,128,128]{2,1,0:T(8,128)S(1)} custom-call(f32[2,64,256]{2,1,0:T(8,128)} %init_ref.1, f32[1,2,64,256]{3,2,1,0:T(8,128)} %guess_ref.1), custom_call_target="tpu_custom_call" | custom-call | tf_op jit(solution)/shard_map/pfasst/pallas_call | solution.py:550
  49.8 0.9 %interleave.1 = f32[1,2,64,256]{3,2,1,0:T(8,128)} custom-call(f32[2,128,128]{2,1,0:T(8,128)S(1)} %pfasst.1.x_ref), custom_call_target="tpu_custom_call" | custom-call | tf_op jit(solution)/shard_map/interleave/pallas_call | solution.py:568

commit v5 on v4

--- a/solution.py
+++ b/solution.py
@@ -316,6 +316,8 @@
     def plane(by, device, wrapped):
         return (message(ic.at[REACH], ic.at[REACH - by], IC, device), wrapped)
 
+    right_guess, left_guess = halo(g, GUESS)
+    launch(low & (c == 0), [left_guess])
     for sender, sign in ((even, 1), (odd, -1)):
         offsets = [sign * by for by in range(1, REACH + 1)]
         launch(sender & low, [plane(by, at(by), (by, False)) for by in offsets[:DEEP]])
@@ -324,7 +326,8 @@
             [plane(by, at(by), None) for by in offsets]
             + [plane(by, at(by, opposite), (by, True)) for by in offsets[:DEEP]],
         )
-    launch(always, halo(g, GUESS))
+    launch(always, [right_guess])
+    launch(high | (c > 0), [left_guess])
     launch(even, [(message(slab(g), slab(f), CORE, up), None)])
     launch(t == 0, [(message(slab(i6), slab(f, -by), SIDES, at(by)), (by, False)) for by in (1, -1)])
     launch(t == 2, [(message(slab(i6), slab(f, -by), SIDES, at(by, 0)), (by, True)) for by in (1, -1)])
@@ -438,7 +441,7 @@
     n_inner = [(copy, (by, False)) for (copy, _), by in zip(n_halo, (1, -1, 1, -1))]
     n_around = [(copy, (by, True)) for (copy, _), by in zip(n_halo, (1, -1, 1, -1))]
     launch(low & edge, n_inner)
-    launch(low & (c == ns - 1), n_around)
+    launch((t == 1) & (c == ns - 1), n_around)
     pl.when(t == 2)(lambda: landed(s.at[DEEP], CROSS))
     launch(
         t == 2,
@@ -458,6 +461,7 @@
         landed(v.at[pl.ds(0, 5), pl.ds(1, 2)], NODES)
 
 
+    launch((t == 0) & (c == ns - 1), n_around)
     crossed = crossing(n2, f2, B_CHUNK, SIDES2)
     launch((t == 1) & later, crossed)
 

time: 50.8 us -> 50.8 us (level)
  no operation moved by 1% of the time
where the time goes in v5:
time: 50.8 us; the launch traced here: 50.6 us
  Pallas kernels  50.6 us (100%)
    pallas_call x1, Pallas kernels, local(): pl.pallas_call(functools.partial(kernel, ns, nt), out_shape=pltpu.VMEM((2...  49.8 us

profile of v5, /device:TPU:1, one launch (start us, length us, event | category | flops | bytes accessed | tf_op | source)
XLA Modules:
  0.0 50.6 jit_solution(5127888049736752756)
XLA Ops:
  0.0 49.8 %pfasst.1.x_ref = f32[2,128,128]{2,1,0:T(8,128)S(1)} custom-call(f32[2,64,256]{2,1,0:T(8,128)} %init_ref.1, f32[1,2,64,256]{3,2,1,0:T(8,128)} %guess_ref.1), custom_call_target="tpu_custom_call" | custom-call | tf_op jit(solution)/shard_map/pfasst/pallas_call | solution.py:554
  49.8 0.9 %interleave.1 = f32[1,2,64,256]{3,2,1,0:T(8,128)} custom-call(f32[2,128,128]{2,1,0:T(8,128)S(1)} %pfasst.1.x_ref), custom_call_target="tpu_custom_call" | custom-call | tf_op jit(solution)/shard_map/interleave/pallas_call | solution.py:572

commit v6 on v5

--- a/solution.py
+++ b/solution.py
@@ -437,7 +437,7 @@
     launch((t == 1) & later, crossed)
 
     n_halo = halo(n2, N2) + halo(n1, N1)
-    launch(high & edge, n_halo)
+    launch(high, n_halo)
     n_inner = [(copy, (by, False)) for (copy, _), by in zip(n_halo, (1, -1, 1, -1))]
     n_around = [(copy, (by, True)) for (copy, _), by in zip(n_halo, (1, -1, 1, -1))]
     launch(low & edge, n_inner)
@@ -447,7 +447,6 @@
         t == 2,
         [(message(s.at[DEEP], s.at[DEEP - by], SPREAD, at(by)), (by, False)) for by in near],
     )
-    launch(high & inland, n_halo)
     drain(first)
 
     @pl.when(even)

time: 50.8 us -> 50.8 us (level)
  no operation moved by 1% of the time
where the time goes in v6:
time: 50.8 us; the launch traced here: 50.6 us
  Pallas kernels  50.6 us (100%)
    pallas_call x1, Pallas kernels, local(): pl.pallas_call(functools.partial(kernel, ns, nt), out_shape=pltpu.VMEM((2...  49.8 us

profile of v6, /device:TPU:1, one launch (start us, length us, event | category | flops | bytes accessed | tf_op | source)
XLA Modules:
  0.0 50.6 jit_solution(1758244516596133578)
XLA Ops:
  0.0 49.8 %pfasst.1.x_ref = f32[2,128,128]{2,1,0:T(8,128)S(1)} custom-call(f32[2,64,256]{2,1,0:T(8,128)} %init_ref.1, f32[1,2,64,256]{3,2,1,0:T(8,128)} %guess_ref.1), custom_call_target="tpu_custom_call" | custom-call | tf_op jit(solution)/shard_map/pfasst/pallas_call | solution.py:553
  49.8 0.9 %interleave.1 = f32[1,2,64,256]{3,2,1,0:T(8,128)} custom-call(f32[2,128,128]{2,1,0:T(8,128)S(1)} %pfasst.1.x_ref), custom_call_target="tpu_custom_call" | custom-call | tf_op jit(solution)/shard_map/interleave/pallas_call | solution.py:571
